TPU v7x, 128 devices: a whole 4x4x4 slice. The times are simulated.
128 devices in a mesh: rollout: 8 (over y, z_hi), tensor: 16 (over x, z_lo, core).
Axes of the slice: x: 4, y: 4, z: 4 (z_hi: 2, z_lo: 2; z = z_hi * 2 + z_lo), core: 2. Of those that a mesh axis runs over, the one named last changes fastest.
Arguments:
- hidden_in: bfloat16 [512, 8192], P('rollout'), may hold values from -6 to 6
- norm_gain: float32 [8192], replicated, may hold values from 0.25 to 1.75
- query_weight_base: bfloat16 [8192, 8192], P(None, 'tensor'), may hold values from -0.0625 to 0.0625
- w_key: bfloat16 [8192, 1024], P(None, 'tensor'), may hold values from -0.0625 to 0.0625
- w_value: bfloat16 [8192, 1024], P(None, 'tensor'), may hold values from -0.0625 to 0.0625
- output_weight_base: bfloat16 [8192, 8192], P('tensor'), may hold values from -0.0625 to 0.0625
- kv_cache: bfloat16 [512, 256, 2, 1024], P(('rollout', 'tensor'))
- cache_lengths: int32 [512], P(('rollout', 'tensor')), may hold values from 1 to 254, as said below
- adapter_shards: bfloat16 [128, 16384], P(('rollout', 'tensor')), may hold values from -0.111328125 to 0.111328125
- shard_order: int32 [128], replicated, may hold values from 0 to 127, each once
Outputs:
- decoded: bfloat16 [2, 512, 8192], P(None, 'rollout', 'tensor')
Inputs may be any that keep to these rules, and one draw needn't show every extreme that they name: `cache_lengths`: row 0 has exactly 254 valid positions and row 1 has 1.
All inputs are finite; a program needn't handle non-finite values.
Results may differ from a plain program's by a relative error of at most 0.019.
Values may be sent and summed in bfloat16 or wider, within the bound.
A program may use at most 128 MiB of HBM per device.

v0:
```python
import jax
import jax.numpy as jnp
from jax import lax
from jax.sharding import PartitionSpec as P

D = 8192
HEADS = 64
KV_HEADS = 8
HEAD_DIM = 128
RANK = 64
STEPS = 2


low_rank_scale = 2.0
norm_epsilon = 1e-05
rope_theta = 500000.0


def rotate(vectors, positions):
    half_dim = HEAD_DIM // 2
    exponent = jnp.arange(half_dim, dtype=jnp.float32) * (2.0 / HEAD_DIM)
    frequency = jnp.float32(rope_theta) ** (-exponent)
    angles = positions.astype(jnp.float32)[:, None, None] * frequency[None, None, :]
    cosine = jnp.cos(angles)
    sine = jnp.sin(angles)
    front_part = vectors[..., :half_dim]
    back_part = vectors[..., half_dim:]
    return jnp.concatenate(
        [front_part * cosine - back_part * sine, back_part * cosine + front_part * sine], axis=-1
    )


def attend_local(query_rot, kv_cache, cache_lengths, keys_all, values_all):
    row_count = query_rot.shape[0]
    capacity = kv_cache.shape[1]
    groups = HEADS // KV_HEADS
    query_heads = query_rot.reshape(row_count, KV_HEADS, groups, HEAD_DIM)
    past_keys = kv_cache[:, :, 0].reshape(row_count, capacity, KV_HEADS, HEAD_DIM)
    past_values = kv_cache[:, :, 1].reshape(row_count, capacity, KV_HEADS, HEAD_DIM)
    score_scale = 1.0 / jnp.sqrt(jnp.float32(HEAD_DIM))
    past_scores = (
        jnp.einsum("rkgd,rpkd->rkgp", query_heads, past_keys, preferred_element_type=jnp.float32)
        * score_scale
    )
    visible = jnp.arange(capacity)[None, :] < cache_lengths[:, None]
    past_scores = jnp.where(visible[:, None, None, :], past_scores, jnp.float32(-1e30))
    fresh_scores = (
        jnp.einsum("rkgd,rskd->rkgs", query_heads, keys_all, preferred_element_type=jnp.float32)
        * score_scale
    )
    scores = jnp.concatenate([past_scores, fresh_scores], axis=-1)
    largest = jnp.max(scores, axis=-1, keepdims=True)
    expo = jnp.exp(scores - largest)
    weights = (expo / jnp.sum(expo, axis=-1, keepdims=True)).astype(jnp.bfloat16)
    attended = jnp.einsum(
        "rkgp,rpkd->rkgd", weights[..., :capacity], past_values, preferred_element_type=jnp.float32
    )
    attended = attended + jnp.einsum(
        "rkgs,rskd->rkgd", weights[..., capacity:], values_all, preferred_element_type=jnp.float32
    )
    return attended.reshape(row_count, HEADS * HEAD_DIM).astype(jnp.bfloat16)


def body(
    hidden_in,
    norm_gain,
    query_weight_base,
    w_key,
    w_value,
    output_weight_base,
    kv_cache,
    cache_lengths,
    adapter_shards,
    shard_order,
):
    everything = lax.all_gather(adapter_shards, ("rollout", "tensor"), axis=0, tiled=True)
    ordered = jnp.zeros_like(everything).at[shard_order].set(everything)
    flattened = ordered.reshape(4, D * RANK)
    query_down_factor = flattened[0].reshape(D, RANK)
    query_up_factor = flattened[1].reshape(RANK, D)
    output_down_factor = flattened[2].reshape(D, RANK)
    output_up_factor = flattened[3].reshape(RANK, D)
    tensor_rank = lax.axis_index("tensor")
    query_cols = query_weight_base.shape[1]
    query_up_factor_local = lax.dynamic_slice_in_dim(
        query_up_factor, tensor_rank * query_cols, query_cols, 1
    )
    output_down_factor_local = lax.dynamic_slice_in_dim(
        output_down_factor, tensor_rank * query_cols, query_cols, 0
    )
    combined_query_weight = (
        query_weight_base.astype(jnp.float32)
        + low_rank_scale
        * jnp.dot(query_down_factor, query_up_factor_local, preferred_element_type=jnp.float32)
    ).astype(jnp.bfloat16)
    combined_output_weight = (
        output_weight_base.astype(jnp.float32)
        + low_rank_scale
        * jnp.dot(output_down_factor_local, output_up_factor, preferred_element_type=jnp.float32)
    ).astype(jnp.bfloat16)
    feature_cols = D // lax.axis_size("tensor")
    stream = hidden_in
    keys_list = []
    values_list = []
    results = []
    for step_index in range(STEPS):
        stream_f = stream.astype(jnp.float32)
        normed = (
            stream_f
            * lax.rsqrt(jnp.mean(stream_f * stream_f, axis=-1, keepdims=True) + norm_epsilon)
            * norm_gain
        ).astype(jnp.bfloat16)
        query = jnp.dot(normed, combined_query_weight, preferred_element_type=jnp.float32).astype(
            jnp.bfloat16
        )
        key_new = jnp.dot(normed, w_key, preferred_element_type=jnp.float32).astype(jnp.bfloat16)
        value_new = jnp.dot(normed, w_value, preferred_element_type=jnp.float32).astype(
            jnp.bfloat16
        )
        query_rows, key_rows, value_rows = (
            lax.all_to_all(query, "tensor", split_axis=0, concat_axis=1, tiled=True),
            lax.all_to_all(key_new, "tensor", split_axis=0, concat_axis=1, tiled=True),
            lax.all_to_all(value_new, "tensor", split_axis=0, concat_axis=1, tiled=True),
        )
        row_count = query_rows.shape[0]
        positions = cache_lengths + step_index
        query_rot = rotate(
            query_rows.astype(jnp.float32).reshape(row_count, HEADS, HEAD_DIM), positions
        ).astype(jnp.bfloat16)
        key_rot = rotate(
            key_rows.astype(jnp.float32).reshape(row_count, KV_HEADS, HEAD_DIM), positions
        ).astype(jnp.bfloat16)
        keys_list.append(key_rot)
        values_list.append(value_rows.reshape(row_count, KV_HEADS, HEAD_DIM))
        keys_all = jnp.stack(keys_list, axis=1)
        values_all = jnp.stack(values_list, axis=1)
        attended = attend_local(query_rot, kv_cache, cache_lengths, keys_all, values_all)
        head_block = lax.all_to_all(attended, "tensor", split_axis=1, concat_axis=0, tiled=True)
        projected = jnp.dot(head_block, combined_output_weight, preferred_element_type=jnp.float32)
        summed = lax.psum(projected, "tensor")
        stream = (stream.astype(jnp.float32) + summed).astype(jnp.bfloat16)
        results.append(
            lax.dynamic_slice_in_dim(stream, tensor_rank * feature_cols, feature_cols, 1)
        )
    return jnp.stack(results, axis=0)


def solution(mesh):
    return jax.shard_map(
        body,
        mesh=mesh,
        in_specs=(
            P("rollout", None),
            P(),
            P(None, "tensor"),
            P(None, "tensor"),
            P(None, "tensor"),
            P("tensor", None),
            P(("rollout", "tensor"), None, None, None),
            P(("rollout", "tensor")),
            P(("rollout", "tensor"), None),
            P(),
        ),
        out_specs=P(None, "rollout", "tensor"),
        check_vma=False,
    )
```

profile of v0, /device:TPU:1, one launch (start us, length us, event | category | flops | bytes accessed | tf_op | source)
XLA Modules:
  0.0 605.9 jit_solution(10466040179011399751)
XLA Ops:
  6.6 0.7 all-gather.3.cloned.1.call-update
  7.3 1.5 fusion.3
  8.8 1.7 convolution_convert_fusion.5
  10.6 0.7 reshape.330
  11.3 7.2 %all-to-all-start.1 = ((bf16[16,2,128]{2,1,0:T(2,128)(2,1)}), bf16[16,2,128]{2,1,0:T(2,128)(2,1)S(1)}, u32[]{:S(2)}, u32[]{:S(2)}) async-start(bf16[16,2,128]{2,1,0:T(2,128)(2,1)} %reshape.330), calls=%async_computation.1 | async-start | bytes 16384 | tf_op jit(solution)/shard_map/all_to_all | solution.py:122
  18.6 0.7 multiply_cosine_fusion
  19.3 1.7 convolution_convert_fusion.4
  21.0 10.0 %fusion.56 = (bf16[4,256,1,1024]{3,2,1,0:T(2,128)(2,1)}, bf16[4,256,1,1024]{3,2,1,0:T(2,128)(2,1)}) fusion(bf16[4,256,2,1024]{3,2,1,0:T(2,128)(2,1)} %param.16), kind=kLoop, calls=%fused_computation.107 | loop fusion | bytes 8388608 | tf_op jit(solution)/shard_map/slice | solution.py:38
  31.1 10.4 %copy.143 = bf16[4,256,1,1024]{1,3,0,2:T(8,128)(2,1)} copy(bf16[4,256,1,1024]{3,2,1,0:T(2,128)(2,1)} %get-tuple-element.11) | data formatting | bytes 4194304
  41.5 0.7 reshape.332
  42.2 8.9 %copy.144 = bf16[4,256,1,1024]{1,3,0,2:T(8,128)(2,1)S(1)} copy(bf16[4,256,1,1024]{3,2,1,0:T(2,128)(2,1)} %get-tuple-element.12) | data formatting | bytes 4194304
  51.1 5.7 all-to-all-start.2
  57.0 5.3 all-to-all-done.2
  62.4 0.6 copy_bitcast_fusion
  63.0 0.7 reshape.311
  63.8 151.4 %all-gather.3.cloned.1.call-done = bf16[128,1,16384]{2,1,0:T(2,128)(2,1)} async-done(((bf16[1,1,16384]{2,1,0:T(2,128)(2,1)}), bf16[128,1,16384]{2,1,0:T(2,128)(2,1)}) %all-gather.3.cloned.1.call-update) | async-done | bytes 4194320 | tf_op jit(solution)/shard_map/all_gather | solution.py:76
  215.2 15.6 %scatter_custom_fusion = bf16[128,16384]{1,0:T(8,128)(2,1)} fusion(s32[128]{0:T(128)S(1)} %compare_select_fusion, bf16[128,1,16384]{2,1,0:T(2,128)(2,1)} %all-gather.3.cloned.1.call-done, bf16[]{:T(256)} %constant.19.clone.1), kind=kCustom, calls=%fused_computation.3 | custom fusion | bytes 8388610 | tf_op jit(solution)/shard_map/scatter | solution.py:77
  230.8 4.3 fusion.55
  235.0 4.0 reshape_squeeze.20
  239.1 2.3 reshape_squeeze.21
  241.3 6.5 %add_convert_fusion.1 = bf16[8192,512]{1,0:T(8,128)(2,1)S(1)} fusion(bf16[8192,512]{1,0:T(8,128)(2,1)} %param.12, bf16[8192,64]{1,0:T(8,128)(2,1)} %reshape_squeeze.20, bf16[64,8192]{1,0:T(8,128)(2,1)} %reshape_squeeze.21, s32[]{:T(128)S(6)} %select_n.17), kind=kOutput, calls=%fused_computation.2 | convolution fusion | flops 553648128 | bytes 18939908 | tf_op jit(solution)/shard_map/dot_general | solution.py:94
  247.8 3.2 copy-done.1
  251.0 1.6 convolution_convert_fusion.1
  252.7 0.7 all_to_all.88
  253.3 5.1 all-to-all-start
  258.5 4.0 reshape_squeeze.24
  262.5 2.2 reshape_squeeze.25
  264.9 0.2 fusion.38
  265.2 2.1 fusion.57
  267.3 0.6 multiply_maximum_fusion
  267.9 1.0 copy.115
  268.9 0.2 fusion.15
  269.4 1.4 fusion.10
  270.8 0.7 copy.119
  271.5 5.7 all-to-all-start.3
  277.2 0.3 all-reduce.3.cloned.1.call-start
  277.5 9.3 %add_convert_fusion = bf16[512,8192]{1,0:T(8,128)(2,1)} fusion(bf16[512,8192]{1,0:T(8,128)(2,1)} %param.15, bf16[64,8192]{1,0:T(8,128)(2,1)} %reshape_squeeze.25, bf16[8192,64]{1,0:T(8,128)(2,1)} %reshape_squeeze.24, s32[]{:T(128)S(6)} %select_n.17), kind=kOutput, calls=%fused_computation.1 | convolution fusion | flops 553648128 | bytes 17956868 | tf_op jit(solution)/shard_map/dot_general | solution.py:99
  286.9 6.3 %fusion.60 = f32[64,8192]{1,0:T(8,128)} fusion(bf16[64,512]{1,0:T(8,128)(2,1)S(1)} %all_to_all.97, bf16[512,8192]{1,0:T(8,128)(2,1)} %add_convert_fusion), kind=kOutput, calls=%fused_computation.111 | convolution fusion | flops 536870912 | bytes 10551296 | tf_op jit(solution)/shard_map/dot_general | solution.py:139
  293.2 0.7 copy-done.10
  294.0 121.5 %all-reduce.3.cloned.1.call-done = f32[64,8192]{1,0:T(8,128)} async-done(((f32[64,8192]{1,0:T(8,128)}), f32[64,8192]{1,0:T(8,128)}) %all-reduce.3.cloned.1.call-update) | async-done | bytes 2097168 | tf_op jit(solution)/shard_map/psum | solution.py:140
  415.5 3.4 fusion.53
  418.9 0.3 multiply_reduce_fusion
  419.2 5.1 convolution_convert_fusion
  424.3 0.5 convolution_convert_fusion.3
  424.9 0.7 reshape.334
  425.6 5.9 all-to-all-start.5
  431.4 2.0 convolution_convert_fusion.2
  433.5 0.7 reshape.336
  434.2 0.6 all_to_all.98
  434.8 2.1 all-to-all-done.5
  436.9 3.9 all-to-all-start.6
  441.0 5.4 all-to-all-done.6
  446.3 4.0 all-to-all-start.4
  450.7 5.6 all-to-all-done.4
  456.4 2.1 fusion.58
  458.5 0.4 fusion.59
  458.9 0.2 fusion.14
  459.5 0.6 fusion.11
  460.2 8.7 %all_to_all.116 = bf16[4,16,512]{2,0,1:T(4,128)(2,1)S(1)} all-to-all(bf16[4,16,512]{2,0,1:T(4,128)(2,1)S(1)} %copy.133), channel_id=1, replica_groups=mesh['rollout'=8,'tensor'=16] {'tensor'}, dimensions={1} | all-to-all | bytes 131072 | tf_op jit(solution)/shard_map/all_to_all | solution.py:138
  469.0 6.3 %fusion.61 = f32[64,8192]{1,0:T(8,128)} fusion(bf16[64,512]{1,0:T(8,128)(2,1)S(1)} %all_to_all.107, bf16[512,8192]{1,0:T(8,128)(2,1)} %add_convert_fusion), kind=kOutput, calls=%fused_computation.112 | convolution fusion | flops 536870912 | bytes 10551296 | tf_op jit(solution)/shard_map/dot_general | solution.py:139
  475.3 0.9 dynamic-slice_bitcast_fusion
  476.2 121.5 %all-reduce.5.cloned.1.call-done = f32[64,8192]{1,0:T(8,128)} async-done(((f32[64,8192]{1,0:T(8,128)}), f32[64,8192]{1,0:T(8,128)}) %all-reduce.5.cloned.1.call-update) | async-done | bytes 2097168 | tf_op jit(solution)/shard_map/psum | solution.py:140
  597.7 1.0 fusion.24
  598.7 0.7 pad_maximum_fusion
  (85 shorter events, 2.4 us)
Async XLA Ops:
  6.5 2.3 copy-start
  6.5 12.7 %copy-start.3 = (bf16[64,8192]{1,0:T(8,128)(2,1)S(1)}, bf16[64,8192]{1,0:T(8,128)(2,1)}, u32[]{:S(2)}) copy-start(bf16[64,8192]{1,0:T(8,128)(2,1)} %param.10) | copy-start | bytes 3145732
  6.5 12.7 %copy-start.5 = (f32[8192]{0:T(1024)S(1)}, f32[8192]{0:T(1024)}, u32[]{:S(2)}) copy-start(f32[8192]{0:T(1024)} %param.11) | copy-start | bytes 98308
  6.5 11.9 %copy-start.16 = (s32[4]{0:T(128)S(1)}, s32[4]{0:T(128)}, u32[]{:S(2)}) copy-start(s32[4]{0:T(128)} %param.17) | copy-start | bytes 52
  6.5 208.7 %all-gather.3.cloned.1.call-start = ((), (), s32[]{:S(2)}) async-start(), calls=%async_computation.10 | async-start | bytes 8454144 | tf_op jit(solution)/shard_map/all_gather | solution.py:76
  11.3 39.8 %all-to-all-start.1 = ((bf16[16,2,128]{2,1,0:T(2,128)(2,1)}), bf16[16,2,128]{2,1,0:T(2,128)(2,1)S(1)}, u32[]{:S(2)}, u32[]{:S(2)}) async-start(bf16[16,2,128]{2,1,0:T(2,128)(2,1)} %reshape.330), calls=%async_computation.1 | async-start | bytes 16384 | tf_op jit(solution)/shard_map/all_to_all | solution.py:122
  18.5 246.6 %copy-start.14 = (pred[4,256]{1,0:T(4,128)(4,1)}, pred[4,256]{1,0:T(4,128)(4,1)S(1)}, u32[]{:S(2)}) copy-start(pred[4,256]{1,0:T(4,128)(4,1)S(1)} %iota_compare_fusion) | copy-start | bytes 3076
  21.0 10.1 %copy-start.17 = (s32[128]{0:T(128)S(1)}, s32[128]{0:T(128)}, u32[]{:S(2)}) copy-start(s32[128]{0:T(128)} %param.19) | copy-start | bytes 1540
  51.1 11.2 %all-to-all-start.2 = ((bf16[16,2,128]{2,1,0:T(2,128)(2,1)}), bf16[16,2,128]{2,1,0:T(2,128)(2,1)S(1)}, u32[]{:S(2)}, u32[]{:S(2)}) async-start(bf16[16,2,128]{2,1,0:T(2,128)(2,1)} %reshape.332), calls=%async_computation.2 | async-start | bytes 16384 | tf_op jit(solution)/shard_map/all_to_all | solution.py:123
  63.8 194.6 %copy-start.7 = (bf16[4,8,64]{2,1,0:T(8,128)(2,1)}, bf16[4,8,64]{2,1,0:T(8,128)(2,1)S(1)}, u32[]{:S(2)}) copy-start(bf16[4,8,64]{2,1,0:T(8,128)(2,1)S(1)} %get-tuple-element.20) | copy-start | bytes 12292
  63.8 194.6 %copy-start.9 = (bf16[4,8,64]{2,1,0:T(8,128)(2,1)}, bf16[4,8,64]{2,1,0:T(8,128)(2,1)S(1)}, u32[]{:S(2)}) copy-start(bf16[4,8,64]{2,1,0:T(8,128)(2,1)S(1)} %get-tuple-element.19) | copy-start | bytes 12292
  241.3 9.7 %copy-start.4 = (bf16[64,8192]{1,0:T(8,128)(2,1)S(1)}, bf16[64,8192]{1,0:T(8,128)(2,1)}, u32[]{:S(2)}) copy-start(bf16[64,8192]{1,0:T(8,128)(2,1)} %param.10) | copy-start | bytes 3145732
  247.8 3.2 copy-start.1
  253.3 11.4 %all-to-all-start = ((bf16[16,4,512]{2,1,0:T(4,128)(2,1)}), bf16[16,4,512]{2,1,0:T(4,128)(2,1)S(1)}, u32[]{:S(2)}, u32[]{:S(2)}) async-start(bf16[16,4,512]{2,1,0:T(4,128)(2,1)} %all_to_all.88), calls=%async_computation | async-start | bytes 131072 | tf_op jit(solution)/shard_map/all_to_all | solution.py:121
  271.5 15.4 %all-to-all-start.3 = ((bf16[4,16,512]{2,0,1:T(4,128)(2,1)}), bf16[4,16,512]{2,0,1:T(4,128)(2,1)S(1)}, u32[]{:S(2)}, u32[]{:S(2)}) async-start(bf16[4,16,512]{2,0,1:T(4,128)(2,1)} %copy.119), calls=%async_computation.3 | async-start | bytes 131072 | tf_op jit(solution)/shard_map/all_to_all | solution.py:138
  277.2 138.3 %all-reduce.3.cloned.1.call-start = ((), (), s32[]{:S(2)}) async-start(), calls=%async_computation.8 | async-start | bytes 4194304 | tf_op jit(solution)/shard_map/psum | solution.py:140
  293.1 0.7 copy-start.10
  293.1 0.7 copy-start.8
  293.1 0.7 copy-start.11
  294.0 125.3 %copy-start.6 = (f32[8192]{0:T(1024)S(1)}, f32[8192]{0:T(1024)}, u32[]{:S(2)}) copy-start(f32[8192]{0:T(1024)} %param.11) | copy-start | bytes 98308
  418.9 5.4 copy-start.2
  424.9 25.5 %copy-start.12 = (f32[4,64]{1,0:T(4,128)S(1)}, f32[4,64]{1,0:T(4,128)}, u32[]{:S(2)}) copy-start(f32[4,64]{1,0:T(4,128)} %get-tuple-element.25) | copy-start | bytes 3076
  424.9 25.5 %copy-start.13 = (f32[4,64]{1,0:T(4,128)S(1)}, f32[4,64]{1,0:T(4,128)}, u32[]{:S(2)}) copy-start(f32[4,64]{1,0:T(4,128)} %get-tuple-element.26) | copy-start | bytes 3076
  425.6 11.4 %all-to-all-start.5 = ((bf16[16,2,128]{2,1,0:T(2,128)(2,1)}), bf16[16,2,128]{2,1,0:T(2,128)(2,1)S(1)}, u32[]{:S(2)}, u32[]{:S(2)}) async-start(bf16[16,2,128]{2,1,0:T(2,128)(2,1)} %reshape.334), calls=%async_computation.5 | async-start | bytes 16384 | tf_op jit(solution)/shard_map/all_to_all | solution.py:122
  431.4 25.0 %copy-start.15 = (pred[4,256]{1,0:T(4,128)(4,1)S(1)}, pred[4,256]{1,0:T(4,128)(4,1)}, u32[]{:S(2)}) copy-start(pred[4,256]{1,0:T(4,128)(4,1)} %copy-done.14) | copy-start | bytes 3076
  436.9 9.4 %all-to-all-start.6 = ((bf16[16,2,128]{2,1,0:T(2,128)(2,1)}), bf16[16,2,128]{2,1,0:T(2,128)(2,1)S(1)}, u32[]{:S(2)}, u32[]{:S(2)}) async-start(bf16[16,2,128]{2,1,0:T(2,128)(2,1)} %reshape.336), calls=%async_computation.6 | async-start | bytes 16384 | tf_op jit(solution)/shard_map/all_to_all | solution.py:123
  446.3 9.9 %all-to-all-start.4 = ((bf16[16,4,512]{2,1,0:T(4,128)(2,1)}), bf16[16,4,512]{2,1,0:T(4,128)(2,1)S(1)}, u32[]{:S(2)}, u32[]{:S(2)}) async-start(bf16[16,4,512]{2,1,0:T(4,128)(2,1)} %all_to_all.98), calls=%async_computation.4 | async-start | bytes 131072 | tf_op jit(solution)/shard_map/all_to_all | solution.py:121
  450.3 147.4 %all-reduce.5.cloned.1.call-start = ((), (), s32[]{:S(2)}) async-start(), calls=%async_computation.9 | async-start | bytes 4194304 | tf_op jit(solution)/shard_map/psum | solution.py:140
Sparse Core Ops, SparseCore 0:
  9.1 206.0 all-gather.2
  293.3 122.1 all-reduce.2
  475.5 122.1 all-reduce.4
where the time goes:
time: 608 us; the launch traced here: 606 us
  waiting for transfers between devices  414 us (68%)
  local copies, waits for them, and re-layouts  74 us (12%)
  matrix products  48.1 us (8%)
  starting transfers between devices  37.8 us (6%)
  between operations  13.6 us (2%)
  other arithmetic  10.3 us (2%)
  blocking collectives  8.72 us (1%)
    psum x2, waiting for transfers between devices, body(): summed = lax.psum(projected, 'tensor')  243 us
    all_gather x1, waiting for transfers between devices, body(): lax.all_gather(adapter_shards, ('rollout', 'tensor'), axis=0, tiled=True)  151 us
    unnamed x46, local copies, waits for them, and re-layouts  26.3 us
    scatter x1, local copies, waits for them, and re-layouts, body(): ordered = jnp.zeros_like(everything).at[shard_order].set(everything)  15.6 us
    all_to_all x2, starting transfers between devices, body(): lax.all_to_all(key_new, 'tensor', split_axis=0, concat_axis=1, tiled=True)  13.1 us
    dot_general x2, matrix products, body(): jnp.dot(head_block, combined_output_weight, preferred_element_type=jnp.fl...  12.6 us
  transfers between devices with their start and end apart: 10, of which 7 were waited for; matrix products, arithmetic and copies ran while one was open for 10% of the time, Pallas kernels for 0%

commit v1 on v0

--- a/solution.py
+++ b/solution.py
@@ -73,21 +73,29 @@
     adapter_shards,
     shard_order,
 ):
-    everything = lax.all_gather(adapter_shards, ("rollout", "tensor"), axis=0, tiled=True)
-    ordered = jnp.zeros_like(everything).at[shard_order].set(everything)
-    flattened = ordered.reshape(4, D * RANK)
-    query_down_factor = flattened[0].reshape(D, RANK)
-    query_up_factor = flattened[1].reshape(RANK, D)
-    output_down_factor = flattened[2].reshape(D, RANK)
-    output_up_factor = flattened[3].reshape(RANK, D)
     tensor_rank = lax.axis_index("tensor")
-    query_cols = query_weight_base.shape[1]
-    query_up_factor_local = lax.dynamic_slice_in_dim(
-        query_up_factor, tensor_rank * query_cols, query_cols, 1
+    me = lax.axis_index("rollout") * 16 + tensor_rank
+    piece = adapter_shards.reshape(16384)
+    is_up = lax.rem(shard_order[me] // 32, 2) == 1
+    chunks = jnp.where(
+        is_up,
+        piece.reshape(2, 16, 512).transpose(1, 0, 2).reshape(16, 1024),
+        piece.reshape(16, 1024),
     )
-    output_down_factor_local = lax.dynamic_slice_in_dim(
-        output_down_factor, tensor_rank * query_cols, query_cols, 0
+    outgoing = jnp.broadcast_to(chunks[None], (8, 16, 1024)).reshape(128, 1024)
+    everything = lax.all_to_all(
+        outgoing, ("rollout", "tensor"), split_axis=0, concat_axis=0, tiled=True
     )
+    ordered = jnp.zeros_like(everything).at[shard_order].set(everything).reshape(4, 32, 1024)
+    query_up_factor_local = ordered[1].reshape(RANK, 512)
+    shared = jnp.stack([ordered[0], ordered[3]])
+    shared = jnp.broadcast_to(shared[None], (16, 2, 32, 1024))
+    shared = lax.all_to_all(shared, "tensor", split_axis=0, concat_axis=0, tiled=True)
+    query_down_factor = shared[:, 0].transpose(1, 0, 2).reshape(D, RANK)
+    output_up_factor = shared[:, 1].reshape(16, RANK, 512).transpose(1, 0, 2).reshape(RANK, D)
+    down = ordered[2].reshape(16, 2, 1024)
+    down = lax.all_to_all(down, "tensor", split_axis=0, concat_axis=0, tiled=True)
+    output_down_factor_local = down.transpose(1, 0, 2).reshape(512, RANK)
     combined_query_weight = (
         query_weight_base.astype(jnp.float32)
         + low_rank_scale
@@ -100,6 +108,7 @@
     ).astype(jnp.bfloat16)
     feature_cols = D // lax.axis_size("tensor")
     stream = hidden_in
+    own = lax.dynamic_slice_in_dim(stream, tensor_rank * feature_cols, feature_cols, 1)
     keys_list = []
     values_list = []
     results = []
@@ -137,11 +146,14 @@
         attended = attend_local(query_rot, kv_cache, cache_lengths, keys_all, values_all)
         head_block = lax.all_to_all(attended, "tensor", split_axis=1, concat_axis=0, tiled=True)
         projected = jnp.dot(head_block, combined_output_weight, preferred_element_type=jnp.float32)
-        summed = lax.psum(projected, "tensor")
-        stream = (stream.astype(jnp.float32) + summed).astype(jnp.bfloat16)
-        results.append(
-            lax.dynamic_slice_in_dim(stream, tensor_rank * feature_cols, feature_cols, 1)
-        )
+        parts = projected.reshape(64, 16, 512).transpose(1, 0, 2)
+        parts = lax.all_to_all(parts, "tensor", split_axis=0, concat_axis=0, tiled=True)
+        own = (own.astype(jnp.float32) + jnp.sum(parts, axis=0)).astype(jnp.bfloat16)
+        results.append(own)
+        if step_index + 1 < STEPS:
+            spread = jnp.broadcast_to(own[None], (16,) + own.shape)
+            spread = lax.all_to_all(spread, "tensor", split_axis=0, concat_axis=0, tiled=True)
+            stream = spread.transpose(1, 0, 2).reshape(64, D)
     return jnp.stack(results, axis=0)
 
 

time: 608 us -> 307 us (0.50)
  waiting for transfers between devices: 414 us -> 75.7 us
  blocking collectives: 8.72 us -> 38.1 us
  starting transfers between devices: 37.8 us -> 64.2 us
  between operations: 13.6 us -> 3.29 us
  matrix products: 48.1 us -> 41.8 us
    psum x2 -> x0, waiting for transfers between devices: 243 us -> none  [body(): summed = lax.psum(projected, 'tensor')]
    all_gather x1 -> x0, waiting for transfers between devices: 151 us -> none  [body(): lax.all_gather(adapter_shards, ('rollout', 'tensor'), axis=0, tiled=True)]
    all_to_all x0 -> x5, waiting for transfers between devices: none -> 51.2 us  [the longest x1 26.9 us: body(): lax.all_to_all(parts, 'tensor', split_axis=0, concat_axis=0, tiled=True)]
    all_to_all x0 -> x5, starting transfers between devices: none -> 33.5 us  [the longest x1 11.5 us: body(): lax.all_to_all(outgoing, ('rollout', 'tensor'), split_axis=0, concat_axis...]
    all_to_all x0 -> x1, blocking collectives: none -> 29.4 us  [body(): lax.all_to_all(parts, 'tensor', split_axis=0, concat_axis=0, tiled=True)]
    scatter x1, local copies, waits for them, and re-layouts: 15.6 us -> 1.27 us  [body(): jnp.zeros_like(everything).at[shard_order].set(everything)]
    dot_general x0 -> x1, local copies, waits for them, and re-layouts: none -> 11.4 us  [body(): jnp.dot(head_block, combined_output_weight, preferred_element_type=jnp.fl...]
    another operation x6, local copies, waits for them, and re-layouts: 14.1 us -> 3.64 us  [the longest x1 2.23 us: body(): shared[:, 1].reshape(16, RANK, 512).transpose(1, 0, 2).reshape(RANK, D)]
  transfers between devices with their start and end apart: 10 -> 12, of which waited for: 7 -> 9; matrix products, arithmetic and copies ran while one was open for 10% -> 26% of each run, Pallas kernels for 0% -> 0%
where the time goes in v1:
time: 307 us; the launch traced here: 305 us
  waiting for transfers between devices  75.7 us (25%)
  local copies, waits for them, and re-layouts  73.6 us (24%)
  starting transfers between devices  64.2 us (21%)
  matrix products  41.8 us (14%)
  blocking collectives  38.1 us (12%)
  other arithmetic  8.42 us (3%)
  between operations  3.29 us (1%)
    all_to_all x1, blocking collectives, body(): lax.all_to_all(parts, 'tensor', split_axis=0, concat_axis=0, tiled=True)  29.4 us
    unnamed x56, local copies, waits for them, and re-layouts  27.1 us
    all_to_all x1, waiting for transfers between devices, body(): lax.all_to_all(parts, 'tensor', split_axis=0, concat_axis=0, tiled=True)  26.9 us
    all_to_all x1, waiting for transfers between devices, body(): lax.all_to_all(spread, 'tensor', split_axis=0, concat_axis=0, tiled=True)  15.5 us
    dot_general x2, matrix products, body(): jnp.dot(head_block, combined_output_weight, preferred_element_type=jnp.fl...  13.3 us
    all_to_all x1, starting transfers between devices, body(): lax.all_to_all(outgoing, ('rollout', 'tensor'), split_axis=0, concat_axis...  11.5 us
    dot_general x1, local copies, waits for them, and re-layouts, body(): jnp.dot(head_block, combined_output_weight, preferred_element_type=jnp.fl...  11.4 us
    all_to_all x2, waiting for transfers between devices, body(): lax.all_to_all(value_new, 'tensor', split_axis=0, concat_axis=1, tiled=True)  10.9 us
  transfers between devices with their start and end apart: 12, of which 9 were waited for; matrix products, arithmetic and copies ran while one was open for 26% of the time, Pallas kernels for 0%

profile of v1, /device:TPU:1, one launch (start us, length us, event | category | flops | bytes accessed | tf_op | source)
XLA Modules:
  0.0 305.1 jit_solution(16776041276228729549)
XLA Ops:
  0.0 1.4 dynamic_slice.7
  4.0 1.0 reduce.6
  5.7 0.8 reduce.10
  6.5 0.9 reshape.373
  7.4 11.5 %all-to-all-start = ((bf16[128,2,512]{2,1,0:T(2,128)(2,1)}), bf16[128,2,512]{2,1,0:T(2,128)(2,1)S(1)}, u32[]{:S(2)}, u32[]{:S(2)}) async-start(bf16[128,2,512]{2,1,0:T(2,128)(2,1)} %reshape.373), calls=%async_computation | async-start | bytes 524288 | tf_op jit(solution)/shard_map/all_to_all | solution.py:86
  20.2 0.7 reshape.371
  20.9 0.7 reshape.375
  21.6 8.7 %all-to-all-done = bf16[128,2,512]{2,1,0:T(2,128)(2,1)S(1)} async-done(((bf16[128,2,512]{2,1,0:T(2,128)(2,1)}), bf16[128,2,512]{2,1,0:T(2,128)(2,1)S(1)}, u32[]{:S(2)}, u32[]{:S(2)}) %all-to-all-start) | async-done | bytes 262176 | tf_op jit(solution)/shard_map/all_to_all | solution.py:86
  30.3 3.7 %all-to-all-start.3 = ((bf16[16,2,128]{2,1,0:T(2,128)(2,1)}), bf16[16,2,128]{2,1,0:T(2,128)(2,1)S(1)}, u32[]{:S(2)}, u32[]{:S(2)}) async-start(bf16[16,2,128]{2,1,0:T(2,128)(2,1)} %reshape.371), calls=%async_computation.3 | async-start | bytes 16384 | tf_op jit(solution)/shard_map/all_to_all | solution.py:131
  34.2 1.3 scatter_custom_fusion
  35.5 3.9 %all-to-all-done.3 = bf16[16,2,128]{2,1,0:T(2,128)(2,1)S(1)} async-done(((bf16[16,2,128]{2,1,0:T(2,128)(2,1)}), bf16[16,2,128]{2,1,0:T(2,128)(2,1)S(1)}, u32[]{:S(2)}, u32[]{:S(2)}) %all-to-all-start.3) | async-done | bytes 8224 | tf_op jit(solution)/shard_map/all_to_all | solution.py:131
  39.4 3.9 %all-to-all-start.4 = ((bf16[16,2,128]{2,1,0:T(2,128)(2,1)}), bf16[16,2,128]{2,1,0:T(2,128)(2,1)S(1)}, u32[]{:S(2)}, u32[]{:S(2)}) async-start(bf16[16,2,128]{2,1,0:T(2,128)(2,1)} %reshape.375), calls=%async_computation.4 | async-start | bytes 16384 | tf_op jit(solution)/shard_map/all_to_all | solution.py:132
  43.3 5.5 %all-to-all-done.4 = bf16[16,2,128]{2,1,0:T(2,128)(2,1)S(1)} async-done(((bf16[16,2,128]{2,1,0:T(2,128)(2,1)}), bf16[16,2,128]{2,1,0:T(2,128)(2,1)S(1)}, u32[]{:S(2)}, u32[]{:S(2)}) %all-to-all-start.4) | async-done | bytes 8224 | tf_op jit(solution)/shard_map/all_to_all | solution.py:132
  48.8 1.6 broadcast_in_dim.30
  50.4 4.8 %all-to-all-start.1 = ((bf16[16,2,32,1024]{3,2,1,0:T(8,128)(2,1)}), bf16[16,2,32,1024]{3,2,1,0:T(8,128)(2,1)}, u32[]{:S(2)}, u32[]{:S(2)}) async-start(bf16[16,2,32,1024]{3,2,1,0:T(8,128)(2,1)} %broadcast_in_dim.30), calls=%async_computation.1 | async-start | bytes 4194304 | tf_op jit(solution)/shard_map/all_to_all | solution.py:93
  55.2 10.1 %fusion.49 = (bf16[4,256,1,1024]{3,2,1,0:T(2,128)(2,1)}, bf16[4,256,1,1024]{3,2,1,0:T(2,128)(2,1)}) fusion(bf16[4,256,2,1024]{3,2,1,0:T(2,128)(2,1)} %param.16), kind=kLoop, calls=%fused_computation.108 | loop fusion | bytes 8388608 | tf_op jit(solution)/shard_map/slice | solution.py:38
  65.4 10.5 %copy.180 = bf16[4,256,1,1024]{1,3,0,2:T(8,128)(2,1)} copy(bf16[4,256,1,1024]{3,2,1,0:T(2,128)(2,1)} %get-tuple-element.5) | data formatting | bytes 4194304
  75.8 8.9 %copy.181 = bf16[4,256,1,1024]{1,3,0,2:T(8,128)(2,1)S(1)} copy(bf16[4,256,1,1024]{3,2,1,0:T(2,128)(2,1)} %get-tuple-element.6) | data formatting | bytes 4194304
  84.9 0.9 multiply_cosine_fusion
  86.0 0.6 copy_bitcast_fusion
  86.6 0.7 reshape.347
  87.4 0.7 reshape_squeeze.20
  88.1 5.8 %all-to-all-start.6 = ((bf16[16,2,1024]{2,1,0:T(2,128)(2,1)}), bf16[16,2,1024]{2,1,0:T(2,128)(2,1)S(1)}, u32[]{:S(2)}, u32[]{:S(2)}) async-start(bf16[16,2,1024]{2,1,0:T(2,128)(2,1)} %reshape_squeeze.20), calls=%async_computation.6 | async-start | bytes 131072 | tf_op jit(solution)/shard_map/all_to_all | solution.py:97
  93.9 2.7 fusion.50
  96.6 1.6 copy.141
  98.2 4.0 %reshape.339 = bf16[8192,64]{1,0:T(8,128)(2,1)} reshape(bf16[32,16,1024]{2,1,0:T(8,128)(2,1)} %copy.141) | data formatting | bytes 2097152 | tf_op jit(solution)/shard_map/reshape | solution.py:94
  102.2 5.9 %add_convert_fusion.1 = bf16[8192,512]{1,0:T(8,128)(2,1)S(1)} fusion(bf16[8192,512]{1,0:T(8,128)(2,1)} %param.12, bf16[8192,64]{1,0:T(8,128)(2,1)} %reshape.339, bf16[64,512]{1,0:T(8,128)(2,1)S(1)} %reshape_squeeze.17), kind=kOutput, calls=%fused_computation.2 | convolution fusion | flops 553648128 | bytes 17891328 | tf_op jit(solution)/shard_map/dot_general | solution.py:102
  108.1 3.2 %copy-done.1 = bf16[8192,512]{1,0:T(8,128)(2,1)} copy-done((bf16[8192,512]{1,0:T(8,128)(2,1)}, bf16[8192,512]{1,0:T(8,128)(2,1)S(1)}, u32[]{:S(2)}) %copy-start.1) | copy-done | bytes 8388632
  111.4 1.6 convolution_convert_fusion.1
  113.0 0.7 all_to_all.115
  113.7 5.7 %all-to-all-start.2 = ((bf16[16,4,512]{2,1,0:T(4,128)(2,1)}), bf16[16,4,512]{2,1,0:T(4,128)(2,1)S(1)}, u32[]{:S(2)}, u32[]{:S(2)}) async-start(bf16[16,4,512]{2,1,0:T(4,128)(2,1)} %all_to_all.115), calls=%async_computation.2 | async-start | bytes 131072 | tf_op jit(solution)/shard_map/all_to_all | solution.py:130
  119.5 0.8 reshape.342
  120.3 2.2 reshape_squeeze.21
  122.6 2.4 copy.183
  125.7 2.1 fusion.52
  128.4 1.0 copy.146
  129.9 1.4 fusion.7
  131.3 0.7 copy.150
  132.0 5.4 %all-to-all-start.5 = ((bf16[4,16,512]{2,0,1:T(4,128)(2,1)}), bf16[4,16,512]{2,0,1:T(4,128)(2,1)S(1)}, u32[]{:S(2)}, u32[]{:S(2)}) async-start(bf16[4,16,512]{2,0,1:T(4,128)(2,1)} %copy.150), calls=%async_computation.5 | async-start | bytes 131072 | tf_op jit(solution)/shard_map/all_to_all | solution.py:147
  137.4 7.0 %fusion = bf16[8192,512]{0,1:T(8,128)(2,1)} fusion(bf16[512,64]{1,0:T(8,128)(2,1)S(1)} %copy-done.8, bf16[64,8192]{1,0:T(8,128)(2,1)} %bitcast.109, bf16[512,8192]{1,0:T(8,128)(2,1)} %param.15), kind=kOutput, calls=%fused_computation.3 | convolution fusion | flops 553648128 | bytes 17891328 | tf_op jit(solution)/shard_map/dot_general | solution.py:107
  144.5 11.4 %copy.178 = bf16[8192,512]{1,0:T(8,128)(2,1)} copy(bf16[8192,512]{0,1:T(8,128)(2,1)} %fusion) | data formatting | bytes 16777216 | tf_op jit(solution)/shard_map/dot_general | solution.py:148
  155.9 7.3 %convolution_bitcast_fusion.1 = f32[16,64,512]{2,1,0:T(8,128)} fusion(bf16[64,512,1]{1,0,2:T(8,128)(2,1)S(1)} %reshape.362, bf16[16,512,512]{2,1,0:T(8,128)(2,1)} %bitcast.102), kind=kOutput, calls=%fused_computation.14 | convolution fusion | flops 536870912 | bytes 10551296 | tf_op jit(solution)/shard_map/dot_general | solution.py:148
  163.2 5.7 %all-to-all-start.7 = ((f32[16,64,512]{2,1,0:T(8,128)}), f32[16,64,512]{2,1,0:T(8,128)S(1)}, u32[]{:S(2)}, u32[]{:S(2)}) async-start(f32[16,64,512]{2,1,0:T(8,128)} %convolution_bitcast_fusion.1), calls=%async_computation.7 | async-start | bytes 4194304 | tf_op jit(solution)/shard_map/all_to_all | solution.py:150
  168.9 26.9 %all-to-all-done.7 = f32[16,64,512]{2,1,0:T(8,128)S(1)} async-done(((f32[16,64,512]{2,1,0:T(8,128)}), f32[16,64,512]{2,1,0:T(8,128)S(1)}, u32[]{:S(2)}, u32[]{:S(2)}) %all-to-all-start.7) | async-done | bytes 2097184 | tf_op jit(solution)/shard_map/all_to_all | solution.py:150
  196.1 0.9 add_convert_fusion.4
  197.0 1.1 broadcast_in_dim.32
  198.1 5.7 %all-to-all-start.8 = ((bf16[16,64,512]{2,1,0:T(8,128)(2,1)}), bf16[16,64,512]{2,1,0:T(8,128)(2,1)S(1)}, u32[]{:S(2)}, u32[]{:S(2)}) async-start(bf16[16,64,512]{2,1,0:T(8,128)(2,1)} %broadcast_in_dim.32), calls=%async_computation.8 | async-start | bytes 2097152 | tf_op jit(solution)/shard_map/all_to_all | solution.py:155
  203.9 15.5 %all-to-all-done.8 = bf16[16,64,512]{2,1,0:T(8,128)(2,1)S(1)} async-done(((bf16[16,64,512]{2,1,0:T(8,128)(2,1)}), bf16[16,64,512]{2,1,0:T(8,128)(2,1)S(1)}, u32[]{:S(2)}, u32[]{:S(2)}) %all-to-all-start.8) | async-done | bytes 1048608 | tf_op jit(solution)/shard_map/all_to_all | solution.py:155
  220.8 4.9 %convolution_convert_fusion = bf16[64,512]{1,0:T(8,128)(2,1)S(1)} fusion(bf16[64,8192]{1,0:T(8,128)(2,1)S(1)} %multiply_convert_fusion, bf16[8192,512]{1,0:T(8,128)(2,1)} %copy-done.1), kind=kOutput, calls=%fused_computation.24 | convolution fusion | flops 536903680 | bytes 9502720 | tf_op jit(solution)/shard_map/dot_general | solution.py:122
  226.2 0.7 reshape.377
  226.9 4.1 %all-to-all-start.10 = ((bf16[16,2,128]{2,1,0:T(2,128)(2,1)}), bf16[16,2,128]{2,1,0:T(2,128)(2,1)S(1)}, u32[]{:S(2)}, u32[]{:S(2)}) async-start(bf16[16,2,128]{2,1,0:T(2,128)(2,1)} %reshape.377), calls=%async_computation.10 | async-start | bytes 16384 | tf_op jit(solution)/shard_map/all_to_all | solution.py:131
  231.4 0.7 all_to_all.128
  232.1 0.7 reshape.379
  232.7 3.8 %all-to-all-done.10 = bf16[16,2,128]{2,1,0:T(2,128)(2,1)S(1)} async-done(((bf16[16,2,128]{2,1,0:T(2,128)(2,1)}), bf16[16,2,128]{2,1,0:T(2,128)(2,1)S(1)}, u32[]{:S(2)}, u32[]{:S(2)}) %all-to-all-start.10) | async-done | bytes 8224 | tf_op jit(solution)/shard_map/all_to_all | solution.py:131
  236.5 3.9 %all-to-all-start.11 = ((bf16[16,2,128]{2,1,0:T(2,128)(2,1)}), bf16[16,2,128]{2,1,0:T(2,128)(2,1)S(1)}, u32[]{:S(2)}, u32[]{:S(2)}) async-start(bf16[16,2,128]{2,1,0:T(2,128)(2,1)} %reshape.379), calls=%async_computation.11 | async-start | bytes 16384 | tf_op jit(solution)/shard_map/all_to_all | solution.py:132
  240.6 5.4 %all-to-all-done.11 = bf16[16,2,128]{2,1,0:T(2,128)(2,1)S(1)} async-done(((bf16[16,2,128]{2,1,0:T(2,128)(2,1)}), bf16[16,2,128]{2,1,0:T(2,128)(2,1)S(1)}, u32[]{:S(2)}, u32[]{:S(2)}) %all-to-all-start.11) | async-done | bytes 8224 | tf_op jit(solution)/shard_map/all_to_all | solution.py:132
  246.0 4.0 %all-to-all-start.9 = ((bf16[16,4,512]{2,1,0:T(4,128)(2,1)}), bf16[16,4,512]{2,1,0:T(4,128)(2,1)S(1)}, u32[]{:S(2)}, u32[]{:S(2)}) async-start(bf16[16,4,512]{2,1,0:T(4,128)(2,1)} %all_to_all.128), calls=%async_computation.9 | async-start | bytes 131072 | tf_op jit(solution)/shard_map/all_to_all | solution.py:130
  250.3 5.6 %all-to-all-done.9 = bf16[16,4,512]{2,1,0:T(4,128)(2,1)S(1)} async-done(((bf16[16,4,512]{2,1,0:T(4,128)(2,1)}), bf16[16,4,512]{2,1,0:T(4,128)(2,1)S(1)}, u32[]{:S(2)}, u32[]{:S(2)}) %all-to-all-start.9) | async-done | bytes 65568 | tf_op jit(solution)/shard_map/all_to_all | solution.py:130
  256.1 2.3 fusion.53
  259.3 0.6 fusion.8
  260.1 8.7 %all_to_all.153 = bf16[4,16,512]{2,0,1:T(4,128)(2,1)S(1)} all-to-all(bf16[4,16,512]{2,0,1:T(4,128)(2,1)S(1)} %copy.168), channel_id=1, replica_groups=mesh['rollout'=8,'tensor'=16] {'tensor'}, dimensions={1} | all-to-all | bytes 131072 | tf_op jit(solution)/shard_map/all_to_all | solution.py:147
  268.8 6.0 %convolution_bitcast_fusion = f32[16,64,512]{2,1,0:T(8,128)S(1)} fusion(bf16[64,512,1]{1,0,2:T(8,128)(2,1)S(1)} %reshape.363, bf16[16,512,512]{2,1,0:T(8,128)(2,1)} %bitcast.103), kind=kOutput, calls=%fused_computation.13 | convolution fusion | flops 536870912 | bytes 10551296 | tf_op jit(solution)/shard_map/dot_general | solution.py:148
  274.8 29.4 %all_to_all.154 = f32[16,64,512]{2,1,0:T(8,128)S(1)} all-to-all(f32[16,64,512]{2,1,0:T(8,128)S(1)} %convolution_bitcast_fusion), channel_id=1, replica_groups=mesh['rollout'=8,'tensor'=16] {'tensor'}, dimensions={0} | all-to-all | bytes 4194304 | tf_op jit(solution)/shard_map/all_to_all | solution.py:150
  304.4 0.7 pad_maximum_fusion.1
  (119 shorter events, 8.9 us)
Async XLA Ops:
  0.0 19.2 %copy-start = (bf16[8192,64]{0,1:T(8,128)(2,1)S(1)}, bf16[8192,64]{0,1:T(8,128)(2,1)}, u32[]{:S(2)}) copy-start(bf16[8192,64]{0,1:T(8,128)(2,1)} %param.13) | copy-start | bytes 3145732
  0.0 18.9 %copy-start.4 = (bf16[64,8192]{1,0:T(8,128)(2,1)S(1)}, bf16[64,8192]{1,0:T(8,128)(2,1)}, u32[]{:S(2)}) copy-start(bf16[64,8192]{1,0:T(8,128)(2,1)} %param.10) | copy-start | bytes 3145732
  0.0 19.2 %copy-start.9 = (f32[8192]{0:T(1024)S(1)}, f32[8192]{0:T(1024)}, u32[]{:S(2)}) copy-start(f32[8192]{0:T(1024)} %param.11) | copy-start | bytes 98308
  7.3 12.4 %copy-start.6 = (bf16[8192,64]{0,1:T(8,128)(2,1)S(1)}, bf16[8192,64]{0,1:T(8,128)(2,1)}, u32[]{:S(2)}) copy-start(bf16[8192,64]{0,1:T(8,128)(2,1)} %param.14) | copy-start | bytes 3145732
  7.4 22.9 %all-to-all-start = ((bf16[128,2,512]{2,1,0:T(2,128)(2,1)}), bf16[128,2,512]{2,1,0:T(2,128)(2,1)S(1)}, u32[]{:S(2)}, u32[]{:S(2)}) async-start(bf16[128,2,512]{2,1,0:T(2,128)(2,1)} %reshape.373), calls=%async_computation | async-start | bytes 524288 | tf_op jit(solution)/shard_map/all_to_all | solution.py:86
  19.2 2.4 copy-start.20
  30.3 9.1 %all-to-all-start.3 = ((bf16[16,2,128]{2,1,0:T(2,128)(2,1)}), bf16[16,2,128]{2,1,0:T(2,128)(2,1)S(1)}, u32[]{:S(2)}, u32[]{:S(2)}) async-start(bf16[16,2,128]{2,1,0:T(2,128)(2,1)} %reshape.371), calls=%async_computation.3 | async-start | bytes 16384 | tf_op jit(solution)/shard_map/all_to_all | solution.py:131
  39.4 9.4 %all-to-all-start.4 = ((bf16[16,2,128]{2,1,0:T(2,128)(2,1)}), bf16[16,2,128]{2,1,0:T(2,128)(2,1)S(1)}, u32[]{:S(2)}, u32[]{:S(2)}) async-start(bf16[16,2,128]{2,1,0:T(2,128)(2,1)} %reshape.375), calls=%async_computation.4 | async-start | bytes 16384 | tf_op jit(solution)/shard_map/all_to_all | solution.py:132
  50.4 37.7 %all-to-all-start.1 = ((bf16[16,2,32,1024]{3,2,1,0:T(8,128)(2,1)}), bf16[16,2,32,1024]{3,2,1,0:T(8,128)(2,1)}, u32[]{:S(2)}, u32[]{:S(2)}) async-start(bf16[16,2,32,1024]{3,2,1,0:T(8,128)(2,1)} %broadcast_in_dim.30), calls=%async_computation.1 | async-start | bytes 4194304 | tf_op jit(solution)/shard_map/all_to_all | solution.py:93
  75.8 8.9 %copy-start.21 = (s32[4]{0:T(128)S(1)}, s32[4]{0:T(128)}, u32[]{:S(2)}) copy-start(s32[4]{0:T(128)} %param.17) | copy-start | bytes 52
  84.7 45.1 %copy-start.2 = (bf16[4,256,1,1024]{1,3,0,2:T(8,128)(2,1)}, bf16[4,256,1,1024]{1,3,0,2:T(8,128)(2,1)S(1)}, u32[]{:S(2)}) copy-start(bf16[4,256,1,1024]{1,3,0,2:T(8,128)(2,1)S(1)} %copy.181) | copy-start | bytes 6291460
  84.9 40.8 %copy-start.18 = (pred[4,256]{1,0:T(4,128)(4,1)}, pred[4,256]{1,0:T(4,128)(4,1)S(1)}, u32[]{:S(2)}) copy-start(pred[4,256]{1,0:T(4,128)(4,1)S(1)} %iota_compare_fusion) | copy-start | bytes 3076
  87.4 32.0 %copy-start.11 = (bf16[4,8,64]{2,1,0:T(8,128)(2,1)}, bf16[4,8,64]{2,1,0:T(8,128)(2,1)S(1)}, u32[]{:S(2)}) copy-start(bf16[4,8,64]{2,1,0:T(8,128)(2,1)S(1)} %get-tuple-element.20) | copy-start | bytes 12292
  87.4 32.0 %copy-start.13 = (bf16[4,8,64]{2,1,0:T(8,128)(2,1)}, bf16[4,8,64]{2,1,0:T(8,128)(2,1)S(1)}, u32[]{:S(2)}) copy-start(bf16[4,8,64]{2,1,0:T(8,128)(2,1)S(1)} %get-tuple-element.19) | copy-start | bytes 12292
  88.1 25.6 %all-to-all-start.6 = ((bf16[16,2,1024]{2,1,0:T(2,128)(2,1)}), bf16[16,2,1024]{2,1,0:T(2,128)(2,1)S(1)}, u32[]{:S(2)}, u32[]{:S(2)}) async-start(bf16[16,2,1024]{2,1,0:T(2,128)(2,1)} %reshape_squeeze.20), calls=%async_computation.6 | async-start | bytes 131072 | tf_op jit(solution)/shard_map/all_to_all | solution.py:97
  102.2 9.2 %copy-start.5 = (bf16[64,8192]{1,0:T(8,128)(2,1)S(1)}, bf16[64,8192]{1,0:T(8,128)(2,1)}, u32[]{:S(2)}) copy-start(bf16[64,8192]{1,0:T(8,128)(2,1)} %param.10) | copy-start | bytes 3145732
  108.1 3.3 %copy-start.1 = (bf16[8192,512]{1,0:T(8,128)(2,1)}, bf16[8192,512]{1,0:T(8,128)(2,1)S(1)}, u32[]{:S(2)}) copy-start(bf16[8192,512]{1,0:T(8,128)(2,1)S(1)} %add_convert_fusion.1) | copy-start | bytes 25165828
  113.7 11.6 %all-to-all-start.2 = ((bf16[16,4,512]{2,1,0:T(4,128)(2,1)}), bf16[16,4,512]{2,1,0:T(4,128)(2,1)S(1)}, u32[]{:S(2)}, u32[]{:S(2)}) async-start(bf16[16,4,512]{2,1,0:T(4,128)(2,1)} %all_to_all.115), calls=%async_computation.2 | async-start | bytes 131072 | tf_op jit(solution)/shard_map/all_to_all | solution.py:130
  129.8 7.7 %copy-start.8 = (bf16[512,64]{1,0:T(8,128)(2,1)S(1)}, bf16[512,64]{1,0:T(8,128)(2,1)}, u32[]{:S(2)}) copy-start(bf16[512,64]{1,0:T(8,128)(2,1)} %reshape.342) | copy-start | bytes 196612
  132.0 23.8 %all-to-all-start.5 = ((bf16[4,16,512]{2,0,1:T(4,128)(2,1)}), bf16[4,16,512]{2,0,1:T(4,128)(2,1)S(1)}, u32[]{:S(2)}, u32[]{:S(2)}) async-start(bf16[4,16,512]{2,0,1:T(4,128)(2,1)} %copy.150), calls=%async_computation.5 | async-start | bytes 131072 | tf_op jit(solution)/shard_map/all_to_all | solution.py:147
  163.2 32.7 %all-to-all-start.7 = ((f32[16,64,512]{2,1,0:T(8,128)}), f32[16,64,512]{2,1,0:T(8,128)S(1)}, u32[]{:S(2)}, u32[]{:S(2)}) async-start(f32[16,64,512]{2,1,0:T(8,128)} %convolution_bitcast_fusion.1), calls=%async_computation.7 | async-start | bytes 4194304 | tf_op jit(solution)/shard_map/all_to_all | solution.py:150
  196.1 7.7 %copy-start.14 = (bf16[4,8,64]{2,1,0:T(8,128)(2,1)S(1)}, bf16[4,8,64]{2,1,0:T(8,128)(2,1)}, u32[]{:S(2)}) copy-start(bf16[4,8,64]{2,1,0:T(8,128)(2,1)} %copy-done.13) | copy-start | bytes 12292
  196.1 7.7 %copy-start.12 = (bf16[4,8,64]{2,1,0:T(8,128)(2,1)S(1)}, bf16[4,8,64]{2,1,0:T(8,128)(2,1)}, u32[]{:S(2)}) copy-start(bf16[4,8,64]{2,1,0:T(8,128)(2,1)} %copy-done.11) | copy-start | bytes 12292
  196.1 7.7 %copy-start.15 = (bf16[4,16,64]{2,1,0:T(8,128)(2,1)S(1)}, bf16[4,16,64]{2,1,0:T(8,128)(2,1)}, u32[]{:S(2)}) copy-start(bf16[4,16,64]{2,1,0:T(8,128)(2,1)} %get-tuple-element.21) | copy-start | bytes 24580
  198.1 21.4 %all-to-all-start.8 = ((bf16[16,64,512]{2,1,0:T(8,128)(2,1)}), bf16[16,64,512]{2,1,0:T(8,128)(2,1)S(1)}, u32[]{:S(2)}, u32[]{:S(2)}) async-start(bf16[16,64,512]{2,1,0:T(8,128)(2,1)} %broadcast_in_dim.32), calls=%async_computation.8 | async-start | bytes 2097152 | tf_op jit(solution)/shard_map/all_to_all | solution.py:155
  219.7 0.8 copy-start.10
  225.7 5.3 %copy-start.7 = (bf16[8192,64]{0,1:T(8,128)(2,1)S(1)}, bf16[8192,64]{0,1:T(8,128)(2,1)}, u32[]{:S(2)}) copy-start(bf16[8192,64]{0,1:T(8,128)(2,1)} %param.14) | copy-start | bytes 3145732
  225.7 24.2 %copy-start.16 = (f32[4,64]{1,0:T(4,128)S(1)}, f32[4,64]{1,0:T(4,128)}, u32[]{:S(2)}) copy-start(f32[4,64]{1,0:T(4,128)} %get-tuple-element.25) | copy-start | bytes 3076
  225.7 24.2 %copy-start.17 = (f32[4,64]{1,0:T(4,128)S(1)}, f32[4,64]{1,0:T(4,128)}, u32[]{:S(2)}) copy-start(f32[4,64]{1,0:T(4,128)} %get-tuple-element.26) | copy-start | bytes 3076
  226.2 29.9 %copy-start.19 = (pred[4,256]{1,0:T(4,128)(4,1)S(1)}, pred[4,256]{1,0:T(4,128)(4,1)}, u32[]{:S(2)}) copy-start(pred[4,256]{1,0:T(4,128)(4,1)} %copy-done.18) | copy-start | bytes 3076
  226.9 9.7 %all-to-all-start.10 = ((bf16[16,2,128]{2,1,0:T(2,128)(2,1)}), bf16[16,2,128]{2,1,0:T(2,128)(2,1)S(1)}, u32[]{:S(2)}, u32[]{:S(2)}) async-start(bf16[16,2,128]{2,1,0:T(2,128)(2,1)} %reshape.377), calls=%async_computation.10 | async-start | bytes 16384 | tf_op jit(solution)/shard_map/all_to_all | solution.py:131
  236.5 9.5 %all-to-all-start.11 = ((bf16[16,2,128]{2,1,0:T(2,128)(2,1)}), bf16[16,2,128]{2,1,0:T(2,128)(2,1)S(1)}, u32[]{:S(2)}, u32[]{:S(2)}) async-start(bf16[16,2,128]{2,1,0:T(2,128)(2,1)} %reshape.379), calls=%async_computation.11 | async-start | bytes 16384 | tf_op jit(solution)/shard_map/all_to_all | solution.py:132
  246.0 9.9 %all-to-all-start.9 = ((bf16[16,4,512]{2,1,0:T(4,128)(2,1)}), bf16[16,4,512]{2,1,0:T(4,128)(2,1)S(1)}, u32[]{:S(2)}, u32[]{:S(2)}) async-start(bf16[16,4,512]{2,1,0:T(4,128)(2,1)} %all_to_all.128), calls=%async_computation.9 | async-start | bytes 131072 | tf_op jit(solution)/shard_map/all_to_all | solution.py:130
  256.1 3.2 %copy-start.3 = (bf16[4,256,1,1024]{1,3,0,2:T(8,128)(2,1)S(1)}, bf16[4,256,1,1024]{1,3,0,2:T(8,128)(2,1)}, u32[]{:S(2)}) copy-start(bf16[4,256,1,1024]{1,3,0,2:T(8,128)(2,1)} %copy-done.2) | copy-start | bytes 6291460

commit v2 on v0

v2 whole, which is shorter than its diff:
```python
import jax
import jax.numpy as jnp
import numpy as np
from jax import lax
from jax.experimental import pallas as pl
from jax.experimental.pallas import tpu as pltpu
from jax.sharding import PartitionSpec as P

D = 8192
HEADS = 64
KV_HEADS = 8
HEAD_DIM = 128
RANK = 64
STEPS = 2
CAP = 256
T = 16
R = 8
CHUNK = D // T

low_rank_scale = 2.0
norm_epsilon = 1e-05
rope_theta = 500000.0
score_scale = 1.0 / np.sqrt(np.float32(HEAD_DIM))

f32 = jnp.float32
bf16 = jnp.bfloat16
MESH = pl.DeviceIdType.MESH


def mm(a, b):
    return jnp.dot(a, b, preferred_element_type=f32)


def mm_t(a, b):
    return lax.dot_general(a, b, (((1,), (1,)), ((), ())), preferred_element_type=f32)


def lanes(shape):
    return lax.broadcasted_iota(jnp.int32, shape, len(shape) - 1)


def swap_halves(x):
    return pltpu.roll(x, 64, len(x.shape) - 1)


def spread_pairs(x, ref):
    low = lanes(x.shape) < 64
    rows = x.shape[0]
    ref[pl.ds(0, rows, stride=2), :] = jnp.where(low, x, 0.0)
    ref[pl.ds(1, rows, stride=2), :] = jnp.where(low, swap_halves(x), 0.0)


def pack_rank(t):
    return t[0:32] + swap_halves(t[32:64])


def unpack_split(total):
    high = total.astype(bf16).astype(f32)
    rest = total - high
    low = lanes(total.shape) < 64
    top = jnp.where(low, high, swap_halves(rest))
    bottom = jnp.where(low, swap_halves(high), rest)
    return jnp.concatenate([top, bottom], axis=0).astype(bf16)


def kernel(
    hid, gain, wq, wk_t, wv_t, wo, kv, lens, freq, piece, order,
    out,
    WQ, WKV, WO, KV, HF, ST0, ST1, NB,
    CP, A1R, A2S, A2R, XF, OF, AE, AP, BQ, BO, AOS, AOR, AOE, AO,
    TS, TR, Q32, QS, QR, QX, KN, VN, AF, AM, AR, AT, TOS, TOR, RSS, RB, OUTF,
    lsem, wosem, a1sem, a2sem, aosem, tsem, qsem, asem, tosem, rssem, agdsem, agfsem, agssem,
):
    me = lax.axis_index("tensor")
    ro = lax.axis_index("rollout")
    core = lax.rem(me, 2)
    chip = me // 2
    sib = me + 1 - 2 * core

    def wait(ref, sem):
        pltpu.make_async_copy(ref, ref, sem).wait()

    def tensor_copy(src, dst, send, recv, peer):
        return pltpu.make_async_remote_copy(
            src_ref=src, dst_ref=dst, send_sem=send, recv_sem=recv,
            device_id={"tensor": peer}, device_id_type=MESH,
        )

    def loop(lo, hi, body):
        def step(k, carry):
            body(k)
            return carry
        lax.fori_loop(lo, hi, step, 0)

    barrier = pltpu.get_barrier_semaphore()
    loop(1, T, lambda k: pl.semaphore_signal(
        barrier, inc=1, device_id={"tensor": lax.rem(me + k, T)}, device_id_type=MESH))
    loop(1, R, lambda k: pl.semaphore_signal(
        barrier, inc=1, device_id={"rollout": lax.rem(ro + k, R)}, device_id_type=MESH))

    for j in range(T):
        pltpu.make_async_copy(wq.at[pl.ds(CHUNK * j, CHUNK), :], WQ.at[j], lsem.at[j]).start()
    pltpu.make_async_copy(wk_t, WKV.at[pl.ds(0, 64), :], lsem.at[16]).start()
    pltpu.make_async_copy(wv_t, WKV.at[pl.ds(64, 64), :], lsem.at[17]).start()
    for i in range(4):
        for g in range(KV_HEADS):
            pltpu.make_async_copy(
                kv.at[i, :, :, pl.ds(HEAD_DIM * g, HEAD_DIM)], KV.at[i, g], lsem.at[19]).start()

    def wo_columns(q, parity):
        return wo.at[:, pl.ds(pl.multiple_of((2 * q + parity) * CHUNK, CHUNK), CHUNK)]

    wo_rows = pl.ds(pl.multiple_of(core * CHUNK, CHUNK), CHUNK)
    loop(0, 8, lambda q: pltpu.make_async_copy(
        wo_columns(q, core), WO.at[q, wo_rows, :], lsem.at[18]).start())

    order_row = order[...]
    mine = jnp.sum(
        jnp.where(lanes((1, 128)) == ro * T + me, order_row, 0), axis=1, keepdims=True)
    is_up = jnp.broadcast_to((mine >> 5) & 1, (128, 128))
    row = lax.broadcasted_iota(jnp.int32, (128, 128), 0)
    up_row = 64 * ((row >> 2) & 1) + 4 * (row >> 3) + (row & 3)
    wanted = jnp.where(is_up == 1, up_row, row)
    pick = jnp.where(lanes((128, 128)) == wanted, 1.0, 0.0).astype(bf16)
    CP[...] = mm(pick, piece[...]).astype(bf16)
    A1R[ro] = CP[...]
    place = jnp.where(row == jnp.broadcast_to(order_row, (128, 128)), 1.0, 0.0).astype(bf16)

    pl.semaphore_wait(barrier, T - 1 + R - 1)

    loop(1, R, lambda k: pltpu.make_async_remote_copy(
        src_ref=CP, dst_ref=A1R.at[ro], send_sem=a1sem.at[0], recv_sem=a1sem.at[1],
        device_id={"rollout": lax.rem(ro + k, R)}, device_id_type=MESH).start())
    loop(0, 8, lambda q: tensor_copy(
        wo_columns(q, 1 - core), WO.at[q, wo_rows, :], wosem.at[0], wosem.at[1], sib).start())

    def permute_hidden(j):
        for c in range(4):
            at = pl.multiple_of(CHUNK * j + 128 * c, 128)
            HF[c] = hid[:, pl.ds(at, 128)].astype(f32)
        for c in range(4):
            for i in range(4):
                ST0[j, 16 * i:16 * i + 16, 128 * c:128 * c + 128] = (
                    HF[c, pl.ds(i, 16, stride=4), :].astype(bf16))
    loop(0, T, permute_hidden)

    AP[...] = jnp.zeros_like(AP)
    Q32[320:512, :] = jnp.zeros((192, 128), f32)

    def square_sum(ST, j, total):
        x = ST[j].astype(f32)
        x = x * x
        return total + (x[:, 0:128] + x[:, 128:256]) + (x[:, 256:384] + x[:, 384:512])

    def normalize(ST, total):
        inv = lax.rsqrt(jnp.sum(total, axis=1, keepdims=True) * (1.0 / D) + norm_epsilon)
        def body(j):
            NB[j] = (ST[j].astype(f32) * inv * gain[j]).astype(bf16)
        loop(0, T, body)

    zero_total = jnp.zeros((64, 128), f32)
    normalize(ST0, lax.fori_loop(0, T, lambda j, t: square_sum(ST0, j, t), zero_total))

    wait(A1R.at[pl.ds(0, R - 1)], a1sem.at[1])
    for r in range(R):
        held = A1R[r].astype(f32).reshape(T, 8, 128)
        OF[:, 8 * r:8 * r + 8, :] = held
    A2S[...] = OF[...].astype(bf16)
    loop(1, T, lambda k: tensor_copy(
        A2S.at[lax.rem(me + k, T)], A2R.at[me], a2sem.at[0], a2sem.at[1],
        lax.rem(me + k, T)).start())
    A2R[me] = A2S[me]
    wait(A2R.at[pl.ds(0, T - 1)], a2sem.at[1])

    arrived = A2R[...].astype(f32).reshape(T, R, 8, 128)
    for r in range(R):
        XF[128 * r:128 * r + 128, :] = arrived[:, r].reshape(128, 128)
    FL = AOE
    for s in range(8):
        FL[pl.ds(s, 128, stride=8), :] = mm(place, XF[pl.ds(s, 128, stride=8), :].astype(bf16))
    spread_pairs(FL[0:256, :], AE)
    for b in range(32):
        AP[b, pl.ds(pl.multiple_of(16 * me, 16), 16), :] = AE[16 * b:16 * b + 16, :].astype(bf16)
    for c in range(4):
        up = FL[pl.ds(256 + c, 64, stride=4), :].astype(bf16)
        BQ[0:64, 128 * c:128 * c + 128] = up
        BQ[64:128, 128 * c:128 * c + 128] = up
        up = FL[pl.ds(768 + c, 64, stride=4), :].astype(bf16)
        BO[0:64, 128 * c:128 * c + 128] = up
        BO[64:128, 128 * c:128 * c + 128] = up
    AOS[...] = FL[512:768, :].astype(bf16).reshape(8, 32, 128)

    def send_rank(s):
        def body(j, acc):
            return acc + mm(NB[j], AP[pl.ds(2 * j, 2)].reshape(CHUNK, 128))
        t = lax.fori_loop(0, T, body, zero_total)
        TS[s] = pack_rank(t).astype(bf16)
        loop(1, T, lambda k: tensor_copy(
            TS.at[s], TR.at[s, me], tsem.at[s, 0], tsem.at[s, 1], lax.rem(me + k, T)).start())
        TR[s, me] = TS[s]

    send_rank(0)
    loop(1, T, lambda k: tensor_copy(
        AOS.at[lax.rem(me + k, T) // 2], AOR.at[me], aosem.at[0], aosem.at[1],
        lax.rem(me + k, T)).start())
    AOR[me] = AOS[chip]

    low_half = lanes((8, 128)) < 64
    sub = lax.broadcasted_iota(jnp.int32, (8, 128), 0) & 3
    lengths = jnp.zeros((8, 128), jnp.int32)
    for i in range(4):
        lengths = jnp.where(sub == i, lens[i], lengths)
    wide = lanes((64, 2 * CAP))

    for s in range(STEPS):
        if s == 0:
            wait(WKV.at[pl.ds(0, 64), :], lsem.at[16])
            wait(WKV.at[pl.ds(64, 64), :], lsem.at[17])

        def project(j, carry):
            q, n = carry
            if s == 0:
                wait(WQ.at[j], lsem.at[j])
            x = NB[j]
            q = q + mm(x, WQ[j])
            n = n + mm_t(x, WKV[:, pl.ds(pl.multiple_of(CHUNK * j, CHUNK), CHUNK)])
            return q, n

        q, new = lax.fori_loop(0, T, project, (jnp.zeros((64, CHUNK), f32), zero_total))
        wait(TR.at[s, pl.ds(0, T - 1)], tsem.at[s, 1])
        rank = jnp.sum(TR[s].astype(f32), axis=0)
        q = q + low_rank_scale * mm(unpack_split(rank), BQ[...])
        for h in range(4):
            Q32[64 * h:64 * h + 64, :] = q[:, 128 * h:128 * h + 128]
        Q32[256:320, :] = new
        for t in range(T):
            QS[s, t] = Q32[pl.ds(t, 32, stride=16), :].astype(bf16)
        loop(1, T, lambda k: tensor_copy(
            QS.at[s, lax.rem(me + k, T)], QR.at[s, me], qsem.at[s, 0], qsem.at[s, 1],
            lax.rem(me + k, T)).start())
        QR[s, me] = QS[s, me]

        angles = (lengths + s).astype(f32) * freq[...]
        cosine = jnp.cos(angles)
        sine = jnp.where(low_half, -jnp.sin(angles), jnp.sin(angles))

        if s == 0:
            wait(AOR.at[pl.ds(0, T - 1)], aosem.at[1])
            blocks = AOR[...].astype(f32).reshape(T, 4, 8, 128)
            for b in range(4):
                XF[128 * b:128 * b + 128, :] = blocks[:, b].reshape(128, 128)
            spread_pairs(XF[0:512, :], AOE)
            AO[...] = AOE[...].astype(bf16)

        wait(QR.at[s, pl.ds(0, T - 1)], qsem.at[s, 1])
        got = QR[s].astype(f32)
        heads = got[:, 0:16].reshape(T, 2, 8, 128)
        heads = heads * cosine + swap_halves(heads) * sine
        QX[...] = heads.astype(bf16).astype(f32).reshape(256, 128)
        fresh = got[:, 16:24].reshape(8, 2, 8, 128)
        even, odd = fresh[:, 0], fresh[:, 1]
        low = lanes(even.shape) < 64
        key = jnp.where(low, even, swap_halves(odd))
        key = key * cosine + swap_halves(key) * sine
        KN[s] = key.astype(bf16).astype(f32).reshape(64, 128)
        VN[s] = jnp.where(low, swap_halves(even), odd).reshape(64, 128)

        if s == 0:
            wait(KV, lsem.at[19])

        def attend(i):
            queries = [QX[pl.ds(32 * g + i, 8, stride=4), :] for g in range(KV_HEADS)]
            scores = jnp.concatenate(
                [mm_t(queries[g].astype(bf16), KV[i, g].reshape(2 * CAP, HEAD_DIM))
                 for g in range(KV_HEADS)], axis=0) * score_scale
            seen = ((wide & 1) == 0) & (wide < 2 * lens[i])
            scores = jnp.where(seen, scores, -1e30)
            rows = jnp.concatenate(queries, axis=0)
            largest = jnp.max(scores, axis=1, keepdims=True)
            news, values = [], []
            for n in range(s + 1):
                k = KN[n, pl.ds(i, 8, stride=8), :]
                v = VN[n, pl.ds(i, 8, stride=8), :]
                k = jnp.broadcast_to(k[:, None, :], (8, 8, 128)).reshape(64, 128)
                values.append(jnp.broadcast_to(v[:, None, :], (8, 8, 128)).reshape(64, 128))
                news.append(jnp.sum(rows * k, axis=1, keepdims=True) * score_scale)
                largest = jnp.maximum(largest, news[-1])
            expo = jnp.exp(scores - largest)
            news = [jnp.exp(x - largest) for x in news]
            total = jnp.sum(expo, axis=1, keepdims=True)
            for x in news:
                total = total + x
            weights = pltpu.roll((expo / total).astype(bf16).astype(f32), 1, 1).astype(bf16)
            result = jnp.concatenate(
                [mm(weights[8 * g:8 * g + 8], KV[i, g].reshape(2 * CAP, HEAD_DIM))
                 for g in range(KV_HEADS)], axis=0)
            for x, v in zip(news, values):
                result = result + (x / total).astype(bf16).astype(f32) * v
            AF[pl.ds(i, 64, stride=4), :] = result

        for i in range(4):
            attend(i)
        AM[s] = AF[...].astype(bf16).reshape(8, 32, 128)
        loop(1, T, lambda k: tensor_copy(
            AM.at[s, lax.rem(me + k, T) // 2], AR.at[s, me], asem.at[s, 0], asem.at[s, 1],
            lax.rem(me + k, T)).start())
        AR[s, me] = AM[s, chip]
        wait(AR.at[s, pl.ds(0, T - 1)], asem.at[s, 1])
        XF[0:512, :] = AR[s].astype(f32).reshape(512, 128)
        for h in range(8):
            for i in range(4):
                AT[16 * i:16 * i + 16, 128 * h:128 * h + 128] = (
                    XF[pl.ds(4 * h + i, 16, stride=32), :].astype(bf16))

        attended = AT[...]
        t = mm(attended, AO[...])
        TOS[s] = pack_rank(t).astype(bf16)
        loop(1, 8, lambda k: tensor_copy(
            TOS.at[s], TOR.at[s, chip], tosem.at[s, 0], tosem.at[s, 1],
            lax.rem(me + 2 * k, T)).start())
        TOR[s, chip] = TOS[s]
        if s == 0:
            wait(WO.at[:, pl.ds(0, CHUNK), :], lsem.at[18])
            wait(WO.at[:, pl.ds(0, CHUNK), :], wosem.at[1])

        def part(k):
            q = lax.rem(chip + k, 8)
            RSS[s, q] = mm(AT[...], WO[q]).astype(bf16)
            tensor_copy(
                RSS.at[s, q], RB.at[s, chip], rssem.at[s, 0], rssem.at[s, 1],
                2 * q + core).start()
        loop(1, 8, part)
        RB[s, chip] = jnp.zeros((64, CHUNK), bf16)
        y = mm(attended, WO[chip])
        y = y + (ST0 if s == 0 else ST1)[me].astype(f32)
        wait(TOR.at[s, pl.ds(0, 7)], tosem.at[s, 1])
        rank = jnp.sum(TOR[s].astype(f32), axis=0)
        y = y + low_rank_scale * mm(unpack_split(rank), BO[...])
        wait(RB.at[s, pl.ds(0, 7)], rssem.at[s, 1])
        for q in range(8):
            y = y + RB[s, q].astype(f32)
        y = y.astype(bf16)

        if s + 1 < STEPS:
            ST1[me] = y
            loop(1, 8, lambda k: tensor_copy(
                ST1.at[me], ST1.at[me], agdsem.at[0, k], agdsem.at[1, k],
                lax.rem(me + 2 * k, T)).start())
            tensor_copy(ST1.at[me], ST1.at[me], agssem.at[0], agssem.at[1], sib).start()
        yf = y.astype(f32)
        for c in range(4):
            for i in range(4):
                OUTF[c, pl.ds(i, 16, stride=4), :] = yf[16 * i:16 * i + 16, 128 * c:128 * c + 128]
        for c in range(4):
            out[s, :, 128 * c:128 * c + 128] = OUTF[c].astype(bf16)

        if s + 1 < STEPS:
            total = square_sum(ST1, me, zero_total)

            def pass_on(k, total):
                j = lax.rem(me + T - 2 * k, T)
                wait(ST1.at[j], agdsem.at[1, k])
                tensor_copy(
                    ST1.at[j], ST1.at[j], agfsem.at[0, k], agfsem.at[1, k], sib).start()
                return square_sum(ST1, j, total)
            total = lax.fori_loop(1, 8, pass_on, total)
            wait(ST1.at[sib], agssem.at[1])
            total = square_sum(ST1, sib, total)

            def take(k, total):
                j = lax.rem(sib + T - 2 * k, T)
                wait(ST1.at[j], agfsem.at[1, k])
                return square_sum(ST1, j, total)
            total = lax.fori_loop(1, 8, take, total)
            normalize(ST1, total)
            send_rank(s + 1)

    wait(A1R.at[pl.ds(0, R - 1)], a1sem.at[0])
    wait(WO.at[:, pl.ds(0, CHUNK), :], wosem.at[0])
    wait(A2S.at[pl.ds(0, T - 1)], a2sem.at[0])
    wait(AOR.at[pl.ds(0, T - 1)], aosem.at[0])
    for s in range(STEPS):
        wait(TR.at[s, pl.ds(0, T - 1)], tsem.at[s, 0])
        wait(QR.at[s, pl.ds(0, T - 1)], qsem.at[s, 0])
        wait(AR.at[s, pl.ds(0, T - 1)], asem.at[s, 0])
        wait(TOR.at[s, pl.ds(0, 7)], tosem.at[s, 0])
        wait(RB.at[s, pl.ds(0, 7)], rssem.at[s, 0])
    loop(1, 8, lambda k: wait(ST1.at[me], agdsem.at[0, k]))
    wait(ST1.at[me], agssem.at[0])
    loop(1, 8, lambda k: wait(ST1.at[me], agfsem.at[0, k]))


def body(
    hidden_in,
    norm_gain,
    query_weight_base,
    w_key,
    w_value,
    output_weight_base,
    kv_cache,
    cache_lengths,
    adapter_shards,
    shard_order,
):
    half_dim = HEAD_DIM // 2
    exponent = np.arange(half_dim, dtype=np.float32) * np.float32(2.0 / HEAD_DIM)
    frequency = np.float32(rope_theta) ** (-exponent)
    freq = jnp.asarray(np.concatenate([frequency, frequency]).reshape(1, HEAD_DIM))
    vmem = pl.BlockSpec(memory_space=pltpu.VMEM)
    smem = pl.BlockSpec(memory_space=pltpu.SMEM)
    hbm = pl.BlockSpec(memory_space=pl.ANY)
    V = pltpu.VMEM
    dma = pltpu.SemaphoreType.DMA
    return pl.pallas_call(
        kernel,
        out_shape=jax.ShapeDtypeStruct((STEPS, 64, CHUNK), bf16),
        in_specs=[vmem, vmem, hbm, hbm, hbm, hbm, hbm, smem, vmem, vmem, vmem],
        out_specs=vmem,
        scratch_shapes=[
            V((T, CHUNK, CHUNK), bf16),
            V((128, D), bf16),
            V((8, 2 * CHUNK, CHUNK), bf16),
            V((4, KV_HEADS, CAP, 2, HEAD_DIM), bf16),
            V((4, 64, 128), f32),
            V((T, 64, CHUNK), bf16),
            V((T, 64, CHUNK), bf16),
            V((T, 64, CHUNK), bf16),
            V((128, 128), bf16),
            V((R, 128, 128), bf16),
            V((T, 64, 128), bf16),
            V((T, 64, 128), bf16),
            V((1024, 128), f32),
            V((T, 64, 128), f32),
            V((512, 128), f32),
            V((32, 256, 128), bf16),
            V((128, CHUNK), bf16),
            V((128, CHUNK), bf16),
            V((8, 32, 128), bf16),
            V((T, 32, 128), bf16),
            V((1024, 128), f32),
            V((1024, 128), bf16),
            V((STEPS, 32, 128), bf16),
            V((STEPS, T, 32, 128), bf16),
            V((512, 128), f32),
            V((STEPS, T, 32, 128), bf16),
            V((STEPS, T, 32, 128), bf16),
            V((256, 128), f32),
            V((STEPS, 64, 128), f32),
            V((STEPS, 64, 128), f32),
            V((256, 128), f32),
            V((STEPS, 8, 32, 128), bf16),
            V((STEPS, T, 32, 128), bf16),
            V((64, 2 * CHUNK), bf16),
            V((STEPS, 32, 128), bf16),
            V((STEPS, 8, 32, 128), bf16),
            V((STEPS, 8, 64, CHUNK), bf16),
            V((STEPS, 8, 64, CHUNK), bf16),
            V((4, 64, 128), f32),
            dma((20,)),
            dma((2,)),
            dma((2,)),
            dma((2,)),
            dma((2,)),
            dma((STEPS, 2)),
            dma((STEPS, 2)),
            dma((STEPS, 2)),
            dma((STEPS, 2)),
            dma((STEPS, 2)),
            dma((2, 8)),
            dma((2, 8)),
            dma((2,)),
        ],
        compiler_params=pltpu.CompilerParams(
            collective_id=0, has_side_effects=True, vmem_limit_bytes=56 * 2**20
        ),
        cost_estimate=pl.CostEstimate(
            flops=5 * 10**9, bytes_accessed=25 * 2**20, transcendentals=10**6
        ),
    )(
        hidden_in,
        norm_gain.reshape(T, 1, CHUNK),
        query_weight_base,
        w_key.T,
        w_value.T,
        output_weight_base,
        kv_cache,
        cache_lengths,
        freq,
        adapter_shards.reshape(128, 128),
        shard_order.reshape(1, 128),
    )


def solution(mesh):
    return jax.shard_map(
        body,
        mesh=mesh,
        in_specs=(
            P("rollout", None),
            P(),
            P(None, "tensor"),
            P(None, "tensor"),
            P(None, "tensor"),
            P("tensor", None),
            P(("rollout", "tensor"), None, None, None),
            P(("rollout", "tensor")),
            P(("rollout", "tensor"), None),
            P(),
        ),
        out_specs=P(None, "rollout", "tensor"),
        check_vma=False,
    )
```

time: 608 us -> 95.8 us (0.16)
  waiting for transfers between devices: 414 us -> 0 us
  Pallas kernels: 0 us -> 92.4 us
  local copies, waits for them, and re-layouts: 74 us -> 1.57 us
  matrix products: 48.1 us -> 0 us
  starting transfers between devices: 37.8 us -> 0 us
  between operations: 13.6 us -> 0.01 us
  blocking collectives: 8.72 us -> 0 us
  other arithmetic: 10.3 us -> 1.63 us
    psum x2 -> x0, waiting for transfers between devices: 243 us -> none  [body(): summed = lax.psum(projected, 'tensor')]
    all_gather x1 -> x0, waiting for transfers between devices: 151 us -> none  [body(): lax.all_gather(adapter_shards, ('rollout', 'tensor'), axis=0, tiled=True)]
    pallas_call x0 -> x1, Pallas kernels: none -> 92.4 us  [body(): pl.pallas_call(kernel, out_shape=jax.ShapeDtypeStruct((STEPS, 64, CHUNK),...]
    dot_general x17 -> x0, matrix products: 48.1 us -> none  [the longest x2 12.6 us: body(): jnp.dot(head_block, combined_output_weight, preferred_element_type=jnp.fl...]
    all_to_all x7 -> x0, starting transfers between devices: 37.4 us -> none  [the longest x2 13.1 us: body(): lax.all_to_all(key_new, 'tensor', split_axis=0, concat_axis=1, tiled=True)]
    unnamed x46 -> x1, local copies, waits for them, and re-layouts: 26.3 us -> 1.57 us
    all_to_all x7 -> x0, waiting for transfers between devices: 18.3 us -> none  [the longest x2 10.7 us: body(): lax.all_to_all(value_new, 'tensor', split_axis=0, concat_axis=1, tiled=True)]
    scatter x1 -> x0, local copies, waits for them, and re-layouts: 15.6 us -> none  [body(): ordered = jnp.zeros_like(everything).at[shard_order].set(everything)]
  transfers between devices with their start and end apart: 10 -> 0, of which waited for: 7 -> 0; matrix products, arithmetic and copies ran while one was open for 10% -> 0% of each run, Pallas kernels for 0% -> 0%
where the time goes in v2:
time: 95.8 us; the launch traced here: 95.6 us
  Pallas kernels  92.4 us (96%)
  other arithmetic  1.63 us (2%)
  local copies, waits for them, and re-layouts  1.57 us (2%)
    pallas_call x1, Pallas kernels, body(): pl.pallas_call(kernel, out_shape=jax.ShapeDtypeStruct((STEPS, 64, CHUNK),...  92.4 us

profile of v2, /device:TPU:1, one launch (start us, length us, event | category | flops | bytes accessed | tf_op | source)
XLA Modules:
  0.0 95.6 jit_solution(6085536973470314756)
XLA Ops:
  0.0 1.6 %reduce = bf16[16384]{0:T(1024)(128)(2,1)} reduce(bf16[1,16384]{1,0:T(2,128)(2,1)} %param.19, bf16[]{:T(256)} %constant.6), dimensions={0}, to_apply=%param.19.reduce_sub_computation | reduce | bytes 65538 | tf_op args[8]
  1.6 92.4 %shard_map.109 = bf16[2,64,512]{2,1,0:T(8,128)(2,1)} custom-call(bf16[64,8192]{1,0:T(8,128)(2,1)} %hid.1, f32[16,1,512]{2,1,0:T(1,128)} %bitcast.8, bf16[8192,512]{1,0:T(8,128)(2,1)} %wq.1, bf16[64,8192]{1,0:T(8,128)(2,1)} %bitcast.5, bf16[64,8192]{1,0:T(8,128)(2,1)} %bitcast.6, bf16[512,8192]{1,0:T(8,128)(2,1)} %wo.1, bf16[4,256,2,1024]{3,2,1,0:T(2,128)(2,1)} %kv.1, ...), custom_call_target="tpu_custom_call" | custom-call | flops 5000000000 | bytes 26214400 | tf_op jit(solution)/shard_map/pallas_call | solution.py:414
  94.1 1.6 %copy.13 = bf16[2,64,512]{2,1,0:T(8,128)(2,1)} copy(bf16[2,64,512]{2,1,0:T(8,128)(2,1)} %shard_map.109) | data formatting | bytes 262144

commit v3 on v2

--- a/solution.py
+++ b/solution.py
@@ -66,10 +66,10 @@
 def kernel(
     hid, gain, wq, wk_t, wv_t, wo, kv, lens, freq, piece, order,
     out,
-    WQ, WKV, WO, KV, HF, ST0, ST1, NB,
-    CP, A1R, A2S, A2R, XF, OF, AE, AP, BQ, BO, AOS, AOR, AOE, AO,
-    TS, TR, Q32, QS, QR, QX, KN, VN, AF, AM, AR, AT, TOS, TOR, RSS, RB, OUTF,
-    lsem, wosem, a1sem, a2sem, aosem, tsem, qsem, asem, tosem, rssem, agdsem, agfsem, agssem,
+    WQ, WKV, WO, KV, HF, ST, NB,
+    PF, CP, A1R, A2S, A2R, XF, OF, AE, AQ, BQ, BO, AOS, AOR, AOE, AO,
+    Q32, QS, QR, QX, KN, VN, AF, AM, AR, AT, TOS, TOR, RSS, RB, OUTF,
+    lsem, wosem, a1sem, a2sem, a3dsem, a3fsem, aosem, qsem, asem, tosem, rssem, agdsem, agfsem,
 ):
     me = lax.axis_index("tensor")
     ro = lax.axis_index("rollout")
@@ -95,11 +95,15 @@
     barrier = pltpu.get_barrier_semaphore()
     loop(1, T, lambda k: pl.semaphore_signal(
         barrier, inc=1, device_id={"tensor": lax.rem(me + k, T)}, device_id_type=MESH))
-    loop(1, R, lambda k: pl.semaphore_signal(
-        barrier, inc=1, device_id={"rollout": lax.rem(ro + k, R)}, device_id_type=MESH))
-
-    for j in range(T):
-        pltpu.make_async_copy(wq.at[pl.ds(CHUNK * j, CHUNK), :], WQ.at[j], lsem.at[j]).start()
+    partner = ro + 1 - 2 * lax.rem(ro, 2)
+    loop(1, 4, lambda k: pl.semaphore_signal(
+        barrier, inc=1, device_id={"rollout": lax.rem(ro + 2 * k, R)}, device_id_type=MESH))
+    pl.semaphore_signal(
+        barrier, inc=1, device_id={"rollout": partner}, device_id_type=MESH)
+
+    for j in range(8):
+        pltpu.make_async_copy(
+            wq.at[pl.ds(4 * j, 4)], WQ.at[pl.ds(4 * j, 4)], lsem.at[0]).start()
     pltpu.make_async_copy(wk_t, WKV.at[pl.ds(0, 64), :], lsem.at[16]).start()
     pltpu.make_async_copy(wv_t, WKV.at[pl.ds(64, 64), :], lsem.at[17]).start()
     for i in range(4):
@@ -122,15 +126,22 @@
     up_row = 64 * ((row >> 2) & 1) + 4 * (row >> 3) + (row & 3)
     wanted = jnp.where(is_up == 1, up_row, row)
     pick = jnp.where(lanes((128, 128)) == wanted, 1.0, 0.0).astype(bf16)
-    CP[...] = mm(pick, piece[...]).astype(bf16)
+    flat = piece[...].astype(f32)
+    for r in range(128):
+        PF[r:r + 1, :] = flat[:, 128 * r:128 * r + 128]
+    CP[...] = mm(pick, PF[...].astype(bf16)).astype(bf16)
     A1R[ro] = CP[...]
     place = jnp.where(row == jnp.broadcast_to(order_row, (128, 128)), 1.0, 0.0).astype(bf16)
 
-    pl.semaphore_wait(barrier, T - 1 + R - 1)
-
-    loop(1, R, lambda k: pltpu.make_async_remote_copy(
-        src_ref=CP, dst_ref=A1R.at[ro], send_sem=a1sem.at[0], recv_sem=a1sem.at[1],
-        device_id={"rollout": lax.rem(ro + k, R)}, device_id_type=MESH).start())
+    pl.semaphore_wait(barrier, T - 1 + 4)
+
+    def rollout_copy(src, slot, sem, peer):
+        return pltpu.make_async_remote_copy(
+            src_ref=src, dst_ref=A1R.at[slot], send_sem=a1sem.at[0, sem],
+            recv_sem=a1sem.at[1, sem], device_id={"rollout": peer}, device_id_type=MESH)
+
+    rollout_copy(CP, ro, 0, partner).start()
+    loop(1, 4, lambda k: rollout_copy(CP, ro, 1, lax.rem(ro + 2 * k, R)).start())
     loop(0, 8, lambda q: tensor_copy(
         wo_columns(q, 1 - core), WO.at[q, wo_rows, :], wosem.at[0], wosem.at[1], sib).start())
 
@@ -140,70 +151,107 @@
             HF[c] = hid[:, pl.ds(at, 128)].astype(f32)
         for c in range(4):
             for i in range(4):
-                ST0[j, 16 * i:16 * i + 16, 128 * c:128 * c + 128] = (
+                ST[0, j, 16 * i:16 * i + 16, 128 * c:128 * c + 128] = (
                     HF[c, pl.ds(i, 16, stride=4), :].astype(bf16))
     loop(0, T, permute_hidden)
 
-    AP[...] = jnp.zeros_like(AP)
     Q32[320:512, :] = jnp.zeros((192, 128), f32)
 
-    def square_sum(ST, j, total):
-        x = ST[j].astype(f32)
+    def square_sum(s, j, total):
+        x = ST[s, j].astype(f32)
         x = x * x
         return total + (x[:, 0:128] + x[:, 128:256]) + (x[:, 256:384] + x[:, 384:512])
 
-    def normalize(ST, total):
+    def normalize(s, total):
         inv = lax.rsqrt(jnp.sum(total, axis=1, keepdims=True) * (1.0 / D) + norm_epsilon)
         def body(j):
-            NB[j] = (ST[j].astype(f32) * inv * gain[j]).astype(bf16)
+            NB[j] = (ST[s, j].astype(f32) * inv * gain[j]).astype(bf16)
         loop(0, T, body)
 
     zero_total = jnp.zeros((64, 128), f32)
-    normalize(ST0, lax.fori_loop(0, T, lambda j, t: square_sum(ST0, j, t), zero_total))
-
-    wait(A1R.at[pl.ds(0, R - 1)], a1sem.at[1])
-    for r in range(R):
-        held = A1R[r].astype(f32).reshape(T, 8, 128)
-        OF[:, 8 * r:8 * r + 8, :] = held
-    A2S[...] = OF[...].astype(bf16)
-    loop(1, T, lambda k: tensor_copy(
-        A2S.at[lax.rem(me + k, T)], A2R.at[me], a2sem.at[0], a2sem.at[1],
-        lax.rem(me + k, T)).start())
-    A2R[me] = A2S[me]
-    wait(A2R.at[pl.ds(0, T - 1)], a2sem.at[1])
-
-    arrived = A2R[...].astype(f32).reshape(T, R, 8, 128)
-    for r in range(R):
-        XF[128 * r:128 * r + 128, :] = arrived[:, r].reshape(128, 128)
+    normalize(0, lax.fori_loop(0, T, lambda j, t: square_sum(0, j, t), zero_total))
+
+    def project_kv(j, new):
+        columns = pl.ds(pl.multiple_of(CHUNK * j, CHUNK), CHUNK)
+        return new + mm_t(NB[j], WKV[:, columns])
+
+    wait(A1R.at[0], a1sem.at[1, 0])
+    loop(1, 4, lambda k: rollout_copy(
+        A1R.at[partner], partner, 2, lax.rem(ro + 2 * k, R)).start())
+
+    for half in range(2):
+        z = lax.rem(ro + half, 2)
+        wait(A1R.at[pl.ds(0, 3)], a1sem.at[1, 1 + half])
+        for y in range(4):
+            held = A1R[2 * y + z].astype(f32).reshape(T, 8, 128)
+            OF[:, 8 * y:8 * y + 8, :] = held
+        A2S[half] = OF[...].astype(bf16)
+        loop(1, T, lambda k: tensor_copy(
+            A2S.at[half, lax.rem(me + k, T)], A2R.at[z, me], a2sem.at[half, 0],
+            a2sem.at[half, 1], lax.rem(me + k, T)).start())
+        A2R[z, me] = A2S[half, me]
+
+    wait(WKV.at[pl.ds(0, 64), :], lsem.at[16])
+    wait(WKV.at[pl.ds(64, 64), :], lsem.at[17])
+    new = lax.fori_loop(0, T, project_kv, zero_total)
+    wait(WQ, lsem.at[0])
+    for half in range(2):
+        wait(A2R.at[0, pl.ds(0, T - 1)], a2sem.at[half, 1])
+
+    for z in range(2):
+        arrived = A2R[z].astype(f32).reshape(T, 4, 8, 128)
+        for y in range(4):
+            r = 2 * y + z
+            XF[128 * r:128 * r + 128, :] = arrived[:, y].reshape(128, 128)
     FL = AOE
     for s in range(8):
         FL[pl.ds(s, 128, stride=8), :] = mm(place, XF[pl.ds(s, 128, stride=8), :].astype(bf16))
     spread_pairs(FL[0:256, :], AE)
-    for b in range(32):
-        AP[b, pl.ds(pl.multiple_of(16 * me, 16), 16), :] = AE[16 * b:16 * b + 16, :].astype(bf16)
+    AQ[me] = (AE[0:256, :] + swap_halves(AE[256:512, :])).astype(bf16)
+    loop(1, 8, lambda k: tensor_copy(
+        AQ.at[me], AQ.at[me], a3dsem.at[0, k], a3dsem.at[1, k], lax.rem(me + 2 * k, T)).start())
+    tensor_copy(AQ.at[me], AQ.at[me], a3fsem.at[0, 0], a3fsem.at[1, 0], sib).start()
     for c in range(4):
-        up = FL[pl.ds(256 + c, 64, stride=4), :].astype(bf16)
-        BQ[0:64, 128 * c:128 * c + 128] = up
-        BQ[64:128, 128 * c:128 * c + 128] = up
+        up = (low_rank_scale * FL[pl.ds(256 + c, 64, stride=4), :]).astype(bf16)
+        none = jnp.zeros_like(up)
+        BQ[0, 0:64, 128 * c:128 * c + 128] = up
+        BQ[0, 64:128, 128 * c:128 * c + 128] = none
+        BQ[1, 0:64, 128 * c:128 * c + 128] = none
+        BQ[1, 64:128, 128 * c:128 * c + 128] = up
         up = FL[pl.ds(768 + c, 64, stride=4), :].astype(bf16)
         BO[0:64, 128 * c:128 * c + 128] = up
         BO[64:128, 128 * c:128 * c + 128] = up
     AOS[...] = FL[512:768, :].astype(bf16).reshape(8, 32, 128)
 
-    def send_rank(s):
-        def body(j, acc):
-            return acc + mm(NB[j], AP[pl.ds(2 * j, 2)].reshape(CHUNK, 128))
-        t = lax.fori_loop(0, T, body, zero_total)
-        TS[s] = pack_rank(t).astype(bf16)
-        loop(1, T, lambda k: tensor_copy(
-            TS.at[s], TR.at[s, me], tsem.at[s, 0], tsem.at[s, 1], lax.rem(me + k, T)).start())
-        TR[s, me] = TS[s]
-
-    send_rank(0)
     loop(1, T, lambda k: tensor_copy(
         AOS.at[lax.rem(me + k, T) // 2], AOR.at[me], aosem.at[0], aosem.at[1],
         lax.rem(me + k, T)).start())
     AOR[me] = AOS[chip]
+
+    def merge(j):
+        strip = pl.ds(pl.multiple_of(16 * j, 16), 16)
+        for half in range(2):
+            for m in range(4):
+                change = mm(AQ[j, 64 * m:64 * m + 64, :], BQ[half]).reshape(4, 16, CHUNK)
+                blocks = pl.ds(16 * half + 4 * m, 4)
+                WQ[blocks, strip, :] = (WQ[blocks, strip, :].astype(f32) + change).astype(bf16)
+
+    def merge_direct(k):
+        j = lax.rem(me + T - 2 * k, T)
+
+        @pl.when(k > 0)
+        def _():
+            wait(AQ.at[j], a3dsem.at[1, k])
+            tensor_copy(AQ.at[j], AQ.at[j], a3fsem.at[0, k], a3fsem.at[1, k], sib).start()
+        merge(j)
+
+    def merge_passed(k):
+        j = lax.rem(sib + T - 2 * k, T)
+        wait(AQ.at[j], a3fsem.at[1, k])
+        merge(j)
+
+    loop(0, 8, merge_direct)
+    loop(0, 8, merge_passed)
 
     low_half = lanes((8, 128)) < 64
     sub = lax.broadcasted_iota(jnp.int32, (8, 128), 0) & 3
@@ -213,23 +261,12 @@
     wide = lanes((64, 2 * CAP))
 
     for s in range(STEPS):
-        if s == 0:
-            wait(WKV.at[pl.ds(0, 64), :], lsem.at[16])
-            wait(WKV.at[pl.ds(64, 64), :], lsem.at[17])
-
-        def project(j, carry):
-            q, n = carry
-            if s == 0:
-                wait(WQ.at[j], lsem.at[j])
-            x = NB[j]
-            q = q + mm(x, WQ[j])
-            n = n + mm_t(x, WKV[:, pl.ds(pl.multiple_of(CHUNK * j, CHUNK), CHUNK)])
-            return q, n
-
-        q, new = lax.fori_loop(0, T, project, (jnp.zeros((64, CHUNK), f32), zero_total))
-        wait(TR.at[s, pl.ds(0, T - 1)], tsem.at[s, 1])
-        rank = jnp.sum(TR[s].astype(f32), axis=0)
-        q = q + low_rank_scale * mm(unpack_split(rank), BQ[...])
+        def project(j, q):
+            return q + mm(NB[j], WQ[pl.ds(2 * j, 2)].reshape(CHUNK, CHUNK))
+
+        if s > 0:
+            new = lax.fori_loop(0, T, project_kv, zero_total)
+        q = lax.fori_loop(0, T, project, jnp.zeros((64, CHUNK), f32))
         for h in range(4):
             Q32[64 * h:64 * h + 64, :] = q[:, 128 * h:128 * h + 128]
         Q32[256:320, :] = new
@@ -332,7 +369,7 @@
         loop(1, 8, part)
         RB[s, chip] = jnp.zeros((64, CHUNK), bf16)
         y = mm(attended, WO[chip])
-        y = y + (ST0 if s == 0 else ST1)[me].astype(f32)
+        y = y + ST[s, me].astype(f32)
         wait(TOR.at[s, pl.ds(0, 7)], tosem.at[s, 1])
         rank = jnp.sum(TOR[s].astype(f32), axis=0)
         y = y + low_rank_scale * mm(unpack_split(rank), BO[...])
@@ -342,11 +379,10 @@
         y = y.astype(bf16)
 
         if s + 1 < STEPS:
-            ST1[me] = y
+            ST[1, me] = y
             loop(1, 8, lambda k: tensor_copy(
-                ST1.at[me], ST1.at[me], agdsem.at[0, k], agdsem.at[1, k],
+                ST.at[1, me], ST.at[1, me], agdsem.at[0, k], agdsem.at[1, k],
                 lax.rem(me + 2 * k, T)).start())
-            tensor_copy(ST1.at[me], ST1.at[me], agssem.at[0], agssem.at[1], sib).start()
         yf = y.astype(f32)
         for c in range(4):
             for i in range(4):
@@ -355,39 +391,40 @@
             out[s, :, 128 * c:128 * c + 128] = OUTF[c].astype(bf16)
 
         if s + 1 < STEPS:
-            total = square_sum(ST1, me, zero_total)
-
             def pass_on(k, total):
                 j = lax.rem(me + T - 2 * k, T)
-                wait(ST1.at[j], agdsem.at[1, k])
+
+                @pl.when(k > 0)
+                def _():
+                    wait(ST.at[1, j], agdsem.at[1, k])
                 tensor_copy(
-                    ST1.at[j], ST1.at[j], agfsem.at[0, k], agfsem.at[1, k], sib).start()
-                return square_sum(ST1, j, total)
-            total = lax.fori_loop(1, 8, pass_on, total)
-            wait(ST1.at[sib], agssem.at[1])
-            total = square_sum(ST1, sib, total)
+                    ST.at[1, j], ST.at[1, j], agfsem.at[0, k], agfsem.at[1, k], sib).start()
+                return square_sum(1, j, total)
+            total = lax.fori_loop(0, 8, pass_on, zero_total)
 
             def take(k, total):
                 j = lax.rem(sib + T - 2 * k, T)
-                wait(ST1.at[j], agfsem.at[1, k])
-                return square_sum(ST1, j, total)
-            total = lax.fori_loop(1, 8, take, total)
-            normalize(ST1, total)
-            send_rank(s + 1)
-
-    wait(A1R.at[pl.ds(0, R - 1)], a1sem.at[0])
+                wait(ST.at[1, j], agfsem.at[1, k])
+                return square_sum(1, j, total)
+            total = lax.fori_loop(0, 8, take, total)
+            normalize(1, total)
+
+    wait(A1R.at[0], a1sem.at[0, 0])
+    wait(A1R.at[pl.ds(0, 3)], a1sem.at[0, 1])
+    wait(A1R.at[pl.ds(0, 3)], a1sem.at[0, 2])
     wait(WO.at[:, pl.ds(0, CHUNK), :], wosem.at[0])
-    wait(A2S.at[pl.ds(0, T - 1)], a2sem.at[0])
+    for half in range(2):
+        wait(A2R.at[0, pl.ds(0, T - 1)], a2sem.at[half, 0])
+    loop(1, 8, lambda k: wait(AQ.at[me], a3dsem.at[0, k]))
+    loop(0, 8, lambda k: wait(AQ.at[me], a3fsem.at[0, k]))
     wait(AOR.at[pl.ds(0, T - 1)], aosem.at[0])
     for s in range(STEPS):
-        wait(TR.at[s, pl.ds(0, T - 1)], tsem.at[s, 0])
         wait(QR.at[s, pl.ds(0, T - 1)], qsem.at[s, 0])
         wait(AR.at[s, pl.ds(0, T - 1)], asem.at[s, 0])
         wait(TOR.at[s, pl.ds(0, 7)], tosem.at[s, 0])
         wait(RB.at[s, pl.ds(0, 7)], rssem.at[s, 0])
-    loop(1, 8, lambda k: wait(ST1.at[me], agdsem.at[0, k]))
-    wait(ST1.at[me], agssem.at[0])
-    loop(1, 8, lambda k: wait(ST1.at[me], agfsem.at[0, k]))
+    loop(1, 8, lambda k: wait(ST.at[1, me], agdsem.at[0, k]))
+    loop(0, 8, lambda k: wait(ST.at[1, me], agfsem.at[0, k]))
 
 
 def body(
@@ -417,30 +454,28 @@
         in_specs=[vmem, vmem, hbm, hbm, hbm, hbm, hbm, smem, vmem, vmem, vmem],
         out_specs=vmem,
         scratch_shapes=[
-            V((T, CHUNK, CHUNK), bf16),
+            V((32, 256, CHUNK), bf16),
             V((128, D), bf16),
             V((8, 2 * CHUNK, CHUNK), bf16),
             V((4, KV_HEADS, CAP, 2, HEAD_DIM), bf16),
             V((4, 64, 128), f32),
+            V((2, T, 64, CHUNK), bf16),
             V((T, 64, CHUNK), bf16),
-            V((T, 64, CHUNK), bf16),
-            V((T, 64, CHUNK), bf16),
+            V((128, 128), f32),
             V((128, 128), bf16),
             V((R, 128, 128), bf16),
-            V((T, 64, 128), bf16),
-            V((T, 64, 128), bf16),
+            V((2, T, 32, 128), bf16),
+            V((2, T, 32, 128), bf16),
             V((1024, 128), f32),
-            V((T, 64, 128), f32),
+            V((T, 32, 128), f32),
             V((512, 128), f32),
-            V((32, 256, 128), bf16),
-            V((128, CHUNK), bf16),
+            V((T, 256, 128), bf16),
+            V((2, 128, CHUNK), bf16),
             V((128, CHUNK), bf16),
             V((8, 32, 128), bf16),
             V((T, 32, 128), bf16),
             V((1024, 128), f32),
             V((1024, 128), bf16),
-            V((STEPS, 32, 128), bf16),
-            V((STEPS, T, 32, 128), bf16),
             V((512, 128), f32),
             V((STEPS, T, 32, 128), bf16),
             V((STEPS, T, 32, 128), bf16),
@@ -458,17 +493,17 @@
             V((4, 64, 128), f32),
             dma((20,)),
             dma((2,)),
+            dma((2, 3)),
+            dma((2, 2)),
+            dma((2, 8)),
+            dma((2, 8)),
             dma((2,)),
-            dma((2,)),
-            dma((2,)),
-            dma((STEPS, 2)),
             dma((STEPS, 2)),
             dma((STEPS, 2)),
             dma((STEPS, 2)),
             dma((STEPS, 2)),
             dma((2, 8)),
             dma((2, 8)),
-            dma((2,)),
         ],
         compiler_params=pltpu.CompilerParams(
             collective_id=0, has_side_effects=True, vmem_limit_bytes=56 * 2**20
@@ -479,14 +514,14 @@
     )(
         hidden_in,
         norm_gain.reshape(T, 1, CHUNK),
-        query_weight_base,
+        query_weight_base.reshape(32, 256, CHUNK),
         w_key.T,
         w_value.T,
         output_weight_base,
         kv_cache,
         cache_lengths,
         freq,
-        adapter_shards.reshape(128, 128),
+        adapter_shards,
         shard_order.reshape(1, 128),
     )
 

time: 95.8 us -> 102 us (1.065)
  Pallas kernels: 92.4 us -> 99.9 us
  other arithmetic: 1.63 us -> 0 us
    pallas_call x1, Pallas kernels: 92.4 us -> 99.9 us  [body(): pl.pallas_call(kernel, out_shape=jax.ShapeDtypeStruct((STEPS, 64, CHUNK),...]
    unnamed x1 -> x0, other arithmetic: 1.63 us -> none
where the time goes in v3:
time: 102 us; the launch traced here: 101 us
  Pallas kernels  99.9 us (98%)
  local copies, waits for them, and re-layouts  1.57 us (2%)
    pallas_call x1, Pallas kernels, body(): pl.pallas_call(kernel, out_shape=jax.ShapeDtypeStruct((STEPS, 64, CHUNK),...  99.9 us

profile of v3, /device:TPU:1, one launch (start us, length us, event | category | flops | bytes accessed | tf_op | source)
XLA Modules:
  0.0 101.5 jit_solution(1505953271616296442)
XLA Ops:
  0.0 99.9 %shard_map.109 = bf16[2,64,512]{2,1,0:T(8,128)(2,1)} custom-call(bf16[64,8192]{1,0:T(8,128)(2,1)} %hid.1, f32[16,1,512]{2,1,0:T(1,128)} %bitcast.8, bf16[32,256,512]{2,1,0:T(8,128)(2,1)} %bitcast.5, bf16[64,8192]{1,0:T(8,128)(2,1)} %bitcast.6, bf16[64,8192]{1,0:T(8,128)(2,1)} %bitcast.7, bf16[512,8192]{1,0:T(8,128)(2,1)} %wo.1, ...), custom_call_target="tpu_custom_call" | custom-call | flops 5000000000 | bytes 26214400 | tf_op jit(solution)/shard_map/pallas_call | solution.py:451
  99.9 1.6 %copy.13 = bf16[2,64,512]{2,1,0:T(8,128)(2,1)} copy(bf16[2,64,512]{2,1,0:T(8,128)(2,1)} %shard_map.109) | data formatting | bytes 262144

commit v4 on v3

--- a/solution.py
+++ b/solution.py
@@ -68,8 +68,8 @@
     out,
     WQ, WKV, WO, KV, HF, ST, NB,
     PF, CP, A1R, A2S, A2R, XF, OF, AE, AQ, BQ, BO, AOS, AOR, AOE, AO,
-    Q32, QS, QR, QX, KN, VN, AF, AM, AR, AT, TOS, TOR, RSS, RB, OUTF,
-    lsem, wosem, a1sem, a2sem, a3dsem, a3fsem, aosem, qsem, asem, tosem, rssem, agdsem, agfsem,
+    Q32, QS, QR, QX, KN, VN, AF, AM, AR, AT, TOS, TOR, RSS, RB, OUTF, SQS, SQR,
+    lsem, wosem, a1sem, a2sem, a3dsem, a3fsem, aosem, qsem, asem, tosem, rssem, agdsem, agfsem, sqsem,
 ):
     me = lax.axis_index("tensor")
     ro = lax.axis_index("rollout")
@@ -95,11 +95,8 @@
     barrier = pltpu.get_barrier_semaphore()
     loop(1, T, lambda k: pl.semaphore_signal(
         barrier, inc=1, device_id={"tensor": lax.rem(me + k, T)}, device_id_type=MESH))
-    partner = ro + 1 - 2 * lax.rem(ro, 2)
-    loop(1, 4, lambda k: pl.semaphore_signal(
-        barrier, inc=1, device_id={"rollout": lax.rem(ro + 2 * k, R)}, device_id_type=MESH))
-    pl.semaphore_signal(
-        barrier, inc=1, device_id={"rollout": partner}, device_id_type=MESH)
+    loop(1, R, lambda k: pl.semaphore_signal(
+        barrier, inc=1, device_id={"rollout": lax.rem(ro + k, R)}, device_id_type=MESH))
 
     for j in range(8):
         pltpu.make_async_copy(
@@ -133,15 +130,16 @@
     A1R[ro] = CP[...]
     place = jnp.where(row == jnp.broadcast_to(order_row, (128, 128)), 1.0, 0.0).astype(bf16)
 
-    pl.semaphore_wait(barrier, T - 1 + 4)
-
-    def rollout_copy(src, slot, sem, peer):
-        return pltpu.make_async_remote_copy(
-            src_ref=src, dst_ref=A1R.at[slot], send_sem=a1sem.at[0, sem],
-            recv_sem=a1sem.at[1, sem], device_id={"rollout": peer}, device_id_type=MESH)
-
-    rollout_copy(CP, ro, 0, partner).start()
-    loop(1, 4, lambda k: rollout_copy(CP, ro, 1, lax.rem(ro + 2 * k, R)).start())
+    pl.semaphore_wait(barrier, T - 1 + R - 1)
+
+    def send_piece(peer, sem):
+        pltpu.make_async_remote_copy(
+            src_ref=CP, dst_ref=A1R.at[ro], send_sem=a1sem.at[0, sem],
+            recv_sem=a1sem.at[1, sem], device_id={"rollout": peer}, device_id_type=MESH).start()
+
+    loop(1, 4, lambda k: send_piece(lax.rem(ro + 2 * k, R), 0))
+    other = ro + 1 - 2 * lax.rem(ro, 2)
+    loop(0, 4, lambda k: send_piece(lax.rem(other + 2 * k, R), 1))
     loop(0, 8, lambda q: tensor_copy(
         wo_columns(q, 1 - core), WO.at[q, wo_rows, :], wosem.at[0], wosem.at[1], sib).start())
 
@@ -169,19 +167,16 @@
         loop(0, T, body)
 
     zero_total = jnp.zeros((64, 128), f32)
+    zero_query = jnp.zeros((64, CHUNK), f32)
     normalize(0, lax.fori_loop(0, T, lambda j, t: square_sum(0, j, t), zero_total))
 
     def project_kv(j, new):
         columns = pl.ds(pl.multiple_of(CHUNK * j, CHUNK), CHUNK)
         return new + mm_t(NB[j], WKV[:, columns])
 
-    wait(A1R.at[0], a1sem.at[1, 0])
-    loop(1, 4, lambda k: rollout_copy(
-        A1R.at[partner], partner, 2, lax.rem(ro + 2 * k, R)).start())
-
     for half in range(2):
         z = lax.rem(ro + half, 2)
-        wait(A1R.at[pl.ds(0, 3)], a1sem.at[1, 1 + half])
+        wait(A1R.at[pl.ds(0, 3 + half)], a1sem.at[1, half])
         for y in range(4):
             held = A1R[2 * y + z].astype(f32).reshape(T, 8, 128)
             OF[:, 8 * y:8 * y + 8, :] = held
@@ -250,8 +245,13 @@
         wait(AQ.at[j], a3fsem.at[1, k])
         merge(j)
 
-    loop(0, 8, merge_direct)
-    loop(0, 8, merge_passed)
+    def merge_both(k):
+        merge_direct(k)
+        merge_passed(k - 2)
+
+    loop(0, 2, merge_direct)
+    loop(2, 8, merge_both)
+    loop(6, 8, merge_passed)
 
     low_half = lanes((8, 128)) < 64
     sub = lax.broadcasted_iota(jnp.int32, (8, 128), 0) & 3
@@ -264,9 +264,8 @@
         def project(j, q):
             return q + mm(NB[j], WQ[pl.ds(2 * j, 2)].reshape(CHUNK, CHUNK))
 
-        if s > 0:
-            new = lax.fori_loop(0, T, project_kv, zero_total)
-        q = lax.fori_loop(0, T, project, jnp.zeros((64, CHUNK), f32))
+        if s == 0:
+            q = lax.fori_loop(0, T, project, zero_query)
         for h in range(4):
             Q32[64 * h:64 * h + 64, :] = q[:, 128 * h:128 * h + 128]
         Q32[256:320, :] = new
@@ -380,6 +379,13 @@
 
         if s + 1 < STEPS:
             ST[1, me] = y
+            squares = y.astype(f32) * y.astype(f32)
+            squares = (squares[:, 0:128] + squares[:, 128:256]) + (
+                squares[:, 256:384] + squares[:, 384:512])
+            SQS[...] = jnp.zeros_like(SQS)
+            SQS[0:1, 0:64] = jnp.sum(squares.T, axis=0, keepdims=True)
+            loop(1, T, lambda k: tensor_copy(
+                SQS, SQR.at[me], sqsem.at[0], sqsem.at[1], lax.rem(me + k, T)).start())
             loop(1, 8, lambda k: tensor_copy(
                 ST.at[1, me], ST.at[1, me], agdsem.at[0, k], agdsem.at[1, k],
                 lax.rem(me + 2 * k, T)).start())
@@ -391,7 +397,18 @@
             out[s, :, 128 * c:128 * c + 128] = OUTF[c].astype(bf16)
 
         if s + 1 < STEPS:
-            def pass_on(k, total):
+            SQR[me] = SQS[...]
+            wait(SQR.at[pl.ds(0, T - 1)], sqsem.at[1])
+            total = jnp.sum(SQR[...], axis=0)[0:1]
+            total = jnp.broadcast_to(total, (128, 128)).T[0:64, 0:1]
+            inv = lax.rsqrt(total * (1.0 / D) + norm_epsilon)
+
+            def take(j, carry):
+                q, new = carry
+                NB[j] = (ST[1, j].astype(f32) * inv * gain[j]).astype(bf16)
+                return project(j, q), project_kv(j, new)
+
+            def take_direct(k, carry):
                 j = lax.rem(me + T - 2 * k, T)
 
                 @pl.when(k > 0)
@@ -399,19 +416,20 @@
                     wait(ST.at[1, j], agdsem.at[1, k])
                 tensor_copy(
                     ST.at[1, j], ST.at[1, j], agfsem.at[0, k], agfsem.at[1, k], sib).start()
-                return square_sum(1, j, total)
-            total = lax.fori_loop(0, 8, pass_on, zero_total)
-
-            def take(k, total):
+                return take(j, carry)
+
+            def take_passed(k, carry):
                 j = lax.rem(sib + T - 2 * k, T)
                 wait(ST.at[1, j], agfsem.at[1, k])
-                return square_sum(1, j, total)
-            total = lax.fori_loop(0, 8, take, total)
-            normalize(1, total)
-
-    wait(A1R.at[0], a1sem.at[0, 0])
-    wait(A1R.at[pl.ds(0, 3)], a1sem.at[0, 1])
-    wait(A1R.at[pl.ds(0, 3)], a1sem.at[0, 2])
+                return take(j, carry)
+
+            carry = lax.fori_loop(0, 2, take_direct, (zero_query, zero_total))
+            carry = lax.fori_loop(
+                2, 8, lambda k, c: take_passed(k - 2, take_direct(k, c)), carry)
+            q, new = lax.fori_loop(6, 8, take_passed, carry)
+
+    wait(A1R.at[pl.ds(0, 3)], a1sem.at[0, 0])
+    wait(A1R.at[pl.ds(0, 4)], a1sem.at[0, 1])
     wait(WO.at[:, pl.ds(0, CHUNK), :], wosem.at[0])
     for half in range(2):
         wait(A2R.at[0, pl.ds(0, T - 1)], a2sem.at[half, 0])
@@ -425,6 +443,7 @@
         wait(RB.at[s, pl.ds(0, 7)], rssem.at[s, 0])
     loop(1, 8, lambda k: wait(ST.at[1, me], agdsem.at[0, k]))
     loop(0, 8, lambda k: wait(ST.at[1, me], agfsem.at[0, k]))
+    wait(SQR.at[pl.ds(0, T - 1)], sqsem.at[0])
 
 
 def body(
@@ -491,9 +510,11 @@
             V((STEPS, 8, 64, CHUNK), bf16),
             V((STEPS, 8, 64, CHUNK), bf16),
             V((4, 64, 128), f32),
+            V((8, 128), f32),
+            V((T, 8, 128), f32),
             dma((20,)),
             dma((2,)),
-            dma((2, 3)),
+            dma((2, 2)),
             dma((2, 2)),
             dma((2, 8)),
             dma((2, 8)),
@@ -504,6 +525,7 @@
             dma((STEPS, 2)),
             dma((2, 8)),
             dma((2, 8)),
+            dma((2,)),
         ],
         compiler_params=pltpu.CompilerParams(
             collective_id=0, has_side_effects=True, vmem_limit_bytes=56 * 2**20

time: 102 us -> 97 us (0.951)
  Pallas kernels: 99.9 us -> 95.3 us
    pallas_call x1, Pallas kernels: 99.9 us -> 95.3 us  [body(): pl.pallas_call(kernel, out_shape=jax.ShapeDtypeStruct((STEPS, 64, CHUNK),...]
where the time goes in v4:
time: 97 us; the launch traced here: 96.9 us
  Pallas kernels  95.3 us (98%)
  local copies, waits for them, and re-layouts  1.57 us (2%)
    pallas_call x1, Pallas kernels, body(): pl.pallas_call(kernel, out_shape=jax.ShapeDtypeStruct((STEPS, 64, CHUNK),...  95.3 us

profile of v4, /device:TPU:1, one launch (start us, length us, event | category | flops | bytes accessed | tf_op | source)
XLA Modules:
  0.0 96.9 jit_solution(14989121335583628495)
XLA Ops:
  0.0 95.3 %shard_map.109 = bf16[2,64,512]{2,1,0:T(8,128)(2,1)} custom-call(bf16[64,8192]{1,0:T(8,128)(2,1)} %hid.1, f32[16,1,512]{2,1,0:T(1,128)} %bitcast.8, bf16[32,256,512]{2,1,0:T(8,128)(2,1)} %bitcast.5, bf16[64,8192]{1,0:T(8,128)(2,1)} %bitcast.6, bf16[64,8192]{1,0:T(8,128)(2,1)} %bitcast.7, bf16[512,8192]{1,0:T(8,128)(2,1)} %wo.1, ...), custom_call_target="tpu_custom_call" | custom-call | flops 5000000000 | bytes 26214400 | tf_op jit(solution)/shard_map/pallas_call | solution.py:470
  95.3 1.6 %copy.13 = bf16[2,64,512]{2,1,0:T(8,128)(2,1)} copy(bf16[2,64,512]{2,1,0:T(8,128)(2,1)} %shard_map.109) | data formatting | bytes 262144

commit v5 on v4

--- a/solution.py
+++ b/solution.py
@@ -188,7 +188,7 @@
 
     wait(WKV.at[pl.ds(0, 64), :], lsem.at[16])
     wait(WKV.at[pl.ds(64, 64), :], lsem.at[17])
-    new = lax.fori_loop(0, T, project_kv, zero_total)
+    new = lax.fori_loop(0, T, project_kv, zero_total, unroll=4)
     wait(WQ, lsem.at[0])
     for half in range(2):
         wait(A2R.at[0, pl.ds(0, T - 1)], a2sem.at[half, 1])
@@ -218,11 +218,6 @@
         BO[64:128, 128 * c:128 * c + 128] = up
     AOS[...] = FL[512:768, :].astype(bf16).reshape(8, 32, 128)
 
-    loop(1, T, lambda k: tensor_copy(
-        AOS.at[lax.rem(me + k, T) // 2], AOR.at[me], aosem.at[0], aosem.at[1],
-        lax.rem(me + k, T)).start())
-    AOR[me] = AOS[chip]
-
     def merge(j):
         strip = pl.ds(pl.multiple_of(16 * j, 16), 16)
         for half in range(2):
@@ -265,7 +260,7 @@
             return q + mm(NB[j], WQ[pl.ds(2 * j, 2)].reshape(CHUNK, CHUNK))
 
         if s == 0:
-            q = lax.fori_loop(0, T, project, zero_query)
+            q = lax.fori_loop(0, T, project, zero_query, unroll=4)
         for h in range(4):
             Q32[64 * h:64 * h + 64, :] = q[:, 128 * h:128 * h + 128]
         Q32[256:320, :] = new
@@ -275,18 +270,15 @@
             QS.at[s, lax.rem(me + k, T)], QR.at[s, me], qsem.at[s, 0], qsem.at[s, 1],
             lax.rem(me + k, T)).start())
         QR[s, me] = QS[s, me]
+        if s == 0:
+            loop(1, T, lambda k: tensor_copy(
+                AOS.at[lax.rem(me + k, T) // 2], AOR.at[me], aosem.at[0], aosem.at[1],
+                lax.rem(me + k, T)).start())
+            AOR[me] = AOS[chip]
 
         angles = (lengths + s).astype(f32) * freq[...]
         cosine = jnp.cos(angles)
         sine = jnp.where(low_half, -jnp.sin(angles), jnp.sin(angles))
-
-        if s == 0:
-            wait(AOR.at[pl.ds(0, T - 1)], aosem.at[1])
-            blocks = AOR[...].astype(f32).reshape(T, 4, 8, 128)
-            for b in range(4):
-                XF[128 * b:128 * b + 128, :] = blocks[:, b].reshape(128, 128)
-            spread_pairs(XF[0:512, :], AOE)
-            AO[...] = AOE[...].astype(bf16)
 
         wait(QR.at[s, pl.ds(0, T - 1)], qsem.at[s, 1])
         got = QR[s].astype(f32)
@@ -326,12 +318,13 @@
             total = jnp.sum(expo, axis=1, keepdims=True)
             for x in news:
                 total = total + x
-            weights = pltpu.roll((expo / total).astype(bf16).astype(f32), 1, 1).astype(bf16)
+            share = 1.0 / total
+            weights = pltpu.roll((expo * share).astype(bf16).astype(f32), 1, 1).astype(bf16)
             result = jnp.concatenate(
                 [mm(weights[8 * g:8 * g + 8], KV[i, g].reshape(2 * CAP, HEAD_DIM))
                  for g in range(KV_HEADS)], axis=0)
             for x, v in zip(news, values):
-                result = result + (x / total).astype(bf16).astype(f32) * v
+                result = result + (x * share).astype(bf16).astype(f32) * v
             AF[pl.ds(i, 64, stride=4), :] = result
 
         for i in range(4):
@@ -341,6 +334,13 @@
             AM.at[s, lax.rem(me + k, T) // 2], AR.at[s, me], asem.at[s, 0], asem.at[s, 1],
             lax.rem(me + k, T)).start())
         AR[s, me] = AM[s, chip]
+        if s == 0:
+            wait(AOR.at[pl.ds(0, T - 1)], aosem.at[1])
+            blocks = AOR[...].astype(f32).reshape(T, 4, 8, 128)
+            for b in range(4):
+                XF[128 * b:128 * b + 128, :] = blocks[:, b].reshape(128, 128)
+            spread_pairs(XF[0:512, :], AOE)
+            AO[...] = AOE[...].astype(bf16)
         wait(AR.at[s, pl.ds(0, T - 1)], asem.at[s, 1])
         XF[0:512, :] = AR[s].astype(f32).reshape(512, 128)
         for h in range(8):
@@ -349,12 +349,6 @@
                     XF[pl.ds(4 * h + i, 16, stride=32), :].astype(bf16))
 
         attended = AT[...]
-        t = mm(attended, AO[...])
-        TOS[s] = pack_rank(t).astype(bf16)
-        loop(1, 8, lambda k: tensor_copy(
-            TOS.at[s], TOR.at[s, chip], tosem.at[s, 0], tosem.at[s, 1],
-            lax.rem(me + 2 * k, T)).start())
-        TOR[s, chip] = TOS[s]
         if s == 0:
             wait(WO.at[:, pl.ds(0, CHUNK), :], lsem.at[18])
             wait(WO.at[:, pl.ds(0, CHUNK), :], wosem.at[1])
@@ -366,6 +360,12 @@
                 RSS.at[s, q], RB.at[s, chip], rssem.at[s, 0], rssem.at[s, 1],
                 2 * q + core).start()
         loop(1, 8, part)
+        t = mm(attended, AO[...])
+        TOS[s] = pack_rank(t).astype(bf16)
+        loop(1, 8, lambda k: tensor_copy(
+            TOS.at[s], TOR.at[s, chip], tosem.at[s, 0], tosem.at[s, 1],
+            lax.rem(me + 2 * k, T)).start())
+        TOR[s, chip] = TOS[s]
         RB[s, chip] = jnp.zeros((64, CHUNK), bf16)
         y = mm(attended, WO[chip])
         y = y + ST[s, me].astype(f32)

time: 97 us -> 96.1 us (level)
  Pallas kernels: 95.3 us -> 94.3 us
where the time goes in v5:
time: 96.1 us; the launch traced here: 95.9 us
  Pallas kernels  94.3 us (98%)
  local copies, waits for them, and re-layouts  1.57 us (2%)
    pallas_call x1, Pallas kernels, body(): pl.pallas_call(kernel, out_shape=jax.ShapeDtypeStruct((STEPS, 64, CHUNK),...  94.3 us

profile of v5, /device:TPU:1, one launch (start us, length us, event | category | flops | bytes accessed | tf_op | source)
XLA Modules:
  0.0 95.9 jit_solution(7872468428382707361)
XLA Ops:
  0.0 94.3 %shard_map.109 = bf16[2,64,512]{2,1,0:T(8,128)(2,1)} custom-call(bf16[64,8192]{1,0:T(8,128)(2,1)} %hid.1, f32[16,1,512]{2,1,0:T(1,128)} %bitcast.8, bf16[32,256,512]{2,1,0:T(8,128)(2,1)} %bitcast.5, bf16[64,8192]{1,0:T(8,128)(2,1)} %bitcast.6, bf16[64,8192]{1,0:T(8,128)(2,1)} %bitcast.7, bf16[512,8192]{1,0:T(8,128)(2,1)} %wo.1, ...), custom_call_target="tpu_custom_call" | custom-call | flops 5000000000 | bytes 26214400 | tf_op jit(solution)/shard_map/pallas_call | solution.py:470
  94.3 1.6 %copy.13 = bf16[2,64,512]{2,1,0:T(8,128)(2,1)} copy(bf16[2,64,512]{2,1,0:T(8,128)(2,1)} %shard_map.109) | data formatting | bytes 262144

commit v6 on v5

--- a/solution.py
+++ b/solution.py
@@ -221,32 +221,29 @@
     def merge(j):
         strip = pl.ds(pl.multiple_of(16 * j, 16), 16)
         for half in range(2):
-            for m in range(4):
-                change = mm(AQ[j, 64 * m:64 * m + 64, :], BQ[half]).reshape(4, 16, CHUNK)
-                blocks = pl.ds(16 * half + 4 * m, 4)
-                WQ[blocks, strip, :] = (WQ[blocks, strip, :].astype(f32) + change).astype(bf16)
-
-    def merge_direct(k):
-        j = lax.rem(me + T - 2 * k, T)
-
-        @pl.when(k > 0)
-        def _():
-            wait(AQ.at[j], a3dsem.at[1, k])
-            tensor_copy(AQ.at[j], AQ.at[j], a3fsem.at[0, k], a3fsem.at[1, k], sib).start()
-        merge(j)
-
-    def merge_passed(k):
-        j = lax.rem(sib + T - 2 * k, T)
-        wait(AQ.at[j], a3fsem.at[1, k])
-        merge(j)
-
-    def merge_both(k):
-        merge_direct(k)
-        merge_passed(k - 2)
-
-    loop(0, 2, merge_direct)
-    loop(2, 8, merge_both)
-    loop(6, 8, merge_passed)
+            blocks = pl.ds(16 * half, 16)
+            for n in range(2):
+                columns = slice(256 * n, 256 * n + 256)
+                change = mm(AQ[j], BQ[half, :, columns]).reshape(16, 16, 256)
+                WQ[blocks, strip, columns] = (
+                    WQ[blocks, strip, columns].astype(f32) + change).astype(bf16)
+
+    def own_side(k):
+        return lax.rem(me + T - 2 * k, T)
+
+    def other_side(k):
+        return lax.rem(sib + T - 2 * k, T)
+
+    def pass_on_strips(k):
+        j = own_side(k)
+        wait(AQ.at[j], a3dsem.at[1, k])
+        tensor_copy(AQ.at[j], AQ.at[j], a3fsem.at[0, k], a3fsem.at[1, k], sib).start()
+
+    merge(me)
+    loop(1, 8, pass_on_strips)
+    loop(1, 8, lambda k: merge(own_side(k)))
+    loop(0, 8, lambda k: wait(AQ.at[other_side(k)], a3fsem.at[1, k]))
+    loop(0, 8, lambda k: merge(other_side(k)))
 
     low_half = lanes((8, 128)) < 64
     sub = lax.broadcasted_iota(jnp.int32, (8, 128), 0) & 3
@@ -389,6 +386,8 @@
             loop(1, 8, lambda k: tensor_copy(
                 ST.at[1, me], ST.at[1, me], agdsem.at[0, k], agdsem.at[1, k],
                 lax.rem(me + 2 * k, T)).start())
+            tensor_copy(
+                ST.at[1, me], ST.at[1, me], agfsem.at[0, 0], agfsem.at[1, 0], sib).start()
         yf = y.astype(f32)
         for c in range(4):
             for i in range(4):
@@ -408,25 +407,18 @@
                 NB[j] = (ST[1, j].astype(f32) * inv * gain[j]).astype(bf16)
                 return project(j, q), project_kv(j, new)
 
-            def take_direct(k, carry):
-                j = lax.rem(me + T - 2 * k, T)
-
-                @pl.when(k > 0)
-                def _():
-                    wait(ST.at[1, j], agdsem.at[1, k])
+            def pass_on_stream(k):
+                j = own_side(k)
+                wait(ST.at[1, j], agdsem.at[1, k])
                 tensor_copy(
                     ST.at[1, j], ST.at[1, j], agfsem.at[0, k], agfsem.at[1, k], sib).start()
-                return take(j, carry)
-
-            def take_passed(k, carry):
-                j = lax.rem(sib + T - 2 * k, T)
-                wait(ST.at[1, j], agfsem.at[1, k])
-                return take(j, carry)
-
-            carry = lax.fori_loop(0, 2, take_direct, (zero_query, zero_total))
+
+            loop(1, 8, pass_on_stream)
             carry = lax.fori_loop(
-                2, 8, lambda k, c: take_passed(k - 2, take_direct(k, c)), carry)
-            q, new = lax.fori_loop(6, 8, take_passed, carry)
+                0, 8, lambda k, c: take(own_side(k), c), (zero_query, zero_total), unroll=4)
+            loop(0, 8, lambda k: wait(ST.at[1, other_side(k)], agfsem.at[1, k]))
+            q, new = lax.fori_loop(
+                0, 8, lambda k, c: take(other_side(k), c), carry, unroll=4)
 
     wait(A1R.at[pl.ds(0, 3)], a1sem.at[0, 0])
     wait(A1R.at[pl.ds(0, 4)], a1sem.at[0, 1])

time: 96.1 us -> 97.2 us (1.011)
  Pallas kernels: 94.3 us -> 95.5 us
    pallas_call x1, Pallas kernels: 94.3 us -> 95.5 us  [body(): pl.pallas_call(kernel, out_shape=jax.ShapeDtypeStruct((STEPS, 64, CHUNK),...]
where the time goes in v6:
time: 97.2 us; the launch traced here: 97.1 us
  Pallas kernels  95.5 us (98%)
  local copies, waits for them, and re-layouts  1.57 us (2%)
    pallas_call x1, Pallas kernels, body(): pl.pallas_call(kernel, out_shape=jax.ShapeDtypeStruct((STEPS, 64, CHUNK),...  95.5 us

profile of v6, /device:TPU:1, one launch (start us, length us, event | category | flops | bytes accessed | tf_op | source)
XLA Modules:
  0.0 97.1 jit_solution(16179074286405849413)
XLA Ops:
  0.0 95.5 %shard_map.109 = bf16[2,64,512]{2,1,0:T(8,128)(2,1)} custom-call(bf16[64,8192]{1,0:T(8,128)(2,1)} %hid.1, f32[16,1,512]{2,1,0:T(1,128)} %bitcast.8, bf16[32,256,512]{2,1,0:T(8,128)(2,1)} %bitcast.5, bf16[64,8192]{1,0:T(8,128)(2,1)} %bitcast.6, bf16[64,8192]{1,0:T(8,128)(2,1)} %bitcast.7, bf16[512,8192]{1,0:T(8,128)(2,1)} %wo.1, ...), custom_call_target="tpu_custom_call" | custom-call | flops 5000000000 | bytes 26214400 | tf_op jit(solution)/shard_map/pallas_call | solution.py:462
  95.5 1.6 %copy.13 = bf16[2,64,512]{2,1,0:T(8,128)(2,1)} copy(bf16[2,64,512]{2,1,0:T(8,128)(2,1)} %shard_map.109) | data formatting | bytes 262144

commit v7 on v6

--- a/solution.py
+++ b/solution.py
@@ -68,7 +68,7 @@
     out,
     WQ, WKV, WO, KV, HF, ST, NB,
     PF, CP, A1R, A2S, A2R, XF, OF, AE, AQ, BQ, BO, AOS, AOR, AOE, AO,
-    Q32, QS, QR, QX, KN, VN, AF, AM, AR, AT, TOS, TOR, RSS, RB, OUTF, SQS, SQR,
+    Q32, QS, QR, QX, KN, VN, AF, AM, AR, AT, TOS, TOR, RSS, RB, OUTF, SQS, SQR, DI, KEYS, VALS,
     lsem, wosem, a1sem, a2sem, a3dsem, a3fsem, aosem, qsem, asem, tosem, rssem, agdsem, agfsem, sqsem,
 ):
     me = lax.axis_index("tensor")
@@ -239,7 +239,16 @@
         wait(AQ.at[j], a3dsem.at[1, k])
         tensor_copy(AQ.at[j], AQ.at[j], a3fsem.at[0, k], a3fsem.at[1, k], sib).start()
 
+    wait(KV, lsem.at[19])
+
+    def part_cache(n):
+        i, g = n // KV_HEADS, lax.rem(n, KV_HEADS)
+        DI[...] = KV[i, g].reshape(2 * CAP, HEAD_DIM).astype(f32)
+        KEYS[i, g] = DI[pl.ds(0, CAP, stride=2), :].astype(bf16)
+        VALS[i, g] = DI[pl.ds(1, CAP, stride=2), :].astype(bf16)
+
     merge(me)
+    loop(0, 4 * KV_HEADS, part_cache)
     loop(1, 8, pass_on_strips)
     loop(1, 8, lambda k: merge(own_side(k)))
     loop(0, 8, lambda k: wait(AQ.at[other_side(k)], a3fsem.at[1, k]))
@@ -250,7 +259,7 @@
     lengths = jnp.zeros((8, 128), jnp.int32)
     for i in range(4):
         lengths = jnp.where(sub == i, lens[i], lengths)
-    wide = lanes((64, 2 * CAP))
+    wide = lanes((64, CAP))
 
     for s in range(STEPS):
         def project(j, q):
@@ -290,16 +299,13 @@
         KN[s] = key.astype(bf16).astype(f32).reshape(64, 128)
         VN[s] = jnp.where(low, swap_halves(even), odd).reshape(64, 128)
 
-        if s == 0:
-            wait(KV, lsem.at[19])
 
         def attend(i):
             queries = [QX[pl.ds(32 * g + i, 8, stride=4), :] for g in range(KV_HEADS)]
             scores = jnp.concatenate(
-                [mm_t(queries[g].astype(bf16), KV[i, g].reshape(2 * CAP, HEAD_DIM))
+                [mm_t(queries[g].astype(bf16), KEYS[i, g])
                  for g in range(KV_HEADS)], axis=0) * score_scale
-            seen = ((wide & 1) == 0) & (wide < 2 * lens[i])
-            scores = jnp.where(seen, scores, -1e30)
+            scores = jnp.where(wide < lens[i], scores, -1e30)
             rows = jnp.concatenate(queries, axis=0)
             largest = jnp.max(scores, axis=1, keepdims=True)
             news, values = [], []
@@ -316,9 +322,9 @@
             for x in news:
                 total = total + x
             share = 1.0 / total
-            weights = pltpu.roll((expo * share).astype(bf16).astype(f32), 1, 1).astype(bf16)
+            weights = (expo * share).astype(bf16)
             result = jnp.concatenate(
-                [mm(weights[8 * g:8 * g + 8], KV[i, g].reshape(2 * CAP, HEAD_DIM))
+                [mm(weights[8 * g:8 * g + 8], VALS[i, g])
                  for g in range(KV_HEADS)], axis=0)
             for x, v in zip(news, values):
                 result = result + (x * share).astype(bf16).astype(f32) * v
@@ -504,6 +510,9 @@
             V((4, 64, 128), f32),
             V((8, 128), f32),
             V((T, 8, 128), f32),
+            V((2 * CAP, HEAD_DIM), f32),
+            V((4, KV_HEADS, CAP, HEAD_DIM), bf16),
+            V((4, KV_HEADS, CAP, HEAD_DIM), bf16),
             dma((20,)),
             dma((2,)),
             dma((2, 2)),

time: 97.2 us -> 93.9 us (0.966)
  Pallas kernels: 95.5 us -> 92.2 us
    pallas_call x1, Pallas kernels: 95.5 us -> 92.2 us  [body(): pl.pallas_call(kernel, out_shape=jax.ShapeDtypeStruct((STEPS, 64, CHUNK),...]
where the time goes in v7:
time: 93.9 us; the launch traced here: 93.7 us
  Pallas kernels  92.2 us (98%)
  local copies, waits for them, and re-layouts  1.57 us (2%)
    pallas_call x1, Pallas kernels, body(): pl.pallas_call(kernel, out_shape=jax.ShapeDtypeStruct((STEPS, 64, CHUNK),...  92.2 us

profile of v7, /device:TPU:1, one launch (start us, length us, event | category | flops | bytes accessed | tf_op | source)
XLA Modules:
  0.0 93.7 jit_solution(10906755032612076544)
XLA Ops:
  0.0 92.2 %shard_map.109 = bf16[2,64,512]{2,1,0:T(8,128)(2,1)} custom-call(bf16[64,8192]{1,0:T(8,128)(2,1)} %hid.1, f32[16,1,512]{2,1,0:T(1,128)} %bitcast.8, bf16[32,256,512]{2,1,0:T(8,128)(2,1)} %bitcast.5, bf16[64,8192]{1,0:T(8,128)(2,1)} %bitcast.6, bf16[64,8192]{1,0:T(8,128)(2,1)} %bitcast.7, bf16[512,8192]{1,0:T(8,128)(2,1)} %wo.1, ...), custom_call_target="tpu_custom_call" | custom-call | flops 5000000000 | bytes 26214400 | tf_op jit(solution)/shard_map/pallas_call | solution.py:468
  92.2 1.6 %copy.13 = bf16[2,64,512]{2,1,0:T(8,128)(2,1)} copy(bf16[2,64,512]{2,1,0:T(8,128)(2,1)} %shard_map.109) | data formatting | bytes 262144

commit v8 on v7

--- a/solution.py
+++ b/solution.py
@@ -66,7 +66,7 @@
 def kernel(
     hid, gain, wq, wk_t, wv_t, wo, kv, lens, freq, piece, order,
     out,
-    WQ, WKV, WO, KV, HF, ST, NB,
+    WQ, WKV, WO, KV, HF, ST, SG, NB,
     PF, CP, A1R, A2S, A2R, XF, OF, AE, AQ, BQ, BO, AOS, AOR, AOE, AO,
     Q32, QS, QR, QX, KN, VN, AF, AM, AR, AT, TOS, TOR, RSS, RB, OUTF, SQS, SQR, DI, KEYS, VALS,
     lsem, wosem, a1sem, a2sem, a3dsem, a3fsem, aosem, qsem, asem, tosem, rssem, agdsem, agfsem, sqsem,
@@ -149,26 +149,26 @@
             HF[c] = hid[:, pl.ds(at, 128)].astype(f32)
         for c in range(4):
             for i in range(4):
-                ST[0, j, 16 * i:16 * i + 16, 128 * c:128 * c + 128] = (
+                ST[j, 16 * i:16 * i + 16, 128 * c:128 * c + 128] = (
                     HF[c, pl.ds(i, 16, stride=4), :].astype(bf16))
     loop(0, T, permute_hidden)
 
     Q32[320:512, :] = jnp.zeros((192, 128), f32)
 
-    def square_sum(s, j, total):
-        x = ST[s, j].astype(f32)
+    def square_sum(j, total):
+        x = ST[j].astype(f32)
         x = x * x
         return total + (x[:, 0:128] + x[:, 128:256]) + (x[:, 256:384] + x[:, 384:512])
 
-    def normalize(s, total):
+    def normalize(total):
         inv = lax.rsqrt(jnp.sum(total, axis=1, keepdims=True) * (1.0 / D) + norm_epsilon)
         def body(j):
-            NB[j] = (ST[s, j].astype(f32) * inv * gain[j]).astype(bf16)
+            NB[j] = (ST[j].astype(f32) * inv * gain[j]).astype(bf16)
         loop(0, T, body)
 
     zero_total = jnp.zeros((64, 128), f32)
     zero_query = jnp.zeros((64, CHUNK), f32)
-    normalize(0, lax.fori_loop(0, T, lambda j, t: square_sum(0, j, t), zero_total))
+    normalize(lax.fori_loop(0, T, square_sum, zero_total))
 
     def project_kv(j, new):
         columns = pl.ds(pl.multiple_of(CHUNK * j, CHUNK), CHUNK)
@@ -356,44 +356,56 @@
             wait(WO.at[:, pl.ds(0, CHUNK), :], lsem.at[18])
             wait(WO.at[:, pl.ds(0, CHUNK), :], wosem.at[1])
 
-        def part(k):
-            q = lax.rem(chip + k, 8)
-            RSS[s, q] = mm(AT[...], WO[q]).astype(bf16)
-            tensor_copy(
-                RSS.at[s, q], RB.at[s, chip], rssem.at[s, 0], rssem.at[s, 1],
-                2 * q + core).start()
-        loop(1, 8, part)
+        halves = [slice(256 * half, 256 * half + 256) for half in range(2)]
+
+        def send_parts(half):
+            def part(k):
+                q = lax.rem(chip + k, 8)
+                RSS[s, half, q] = mm(AT[...], WO[q, :, halves[half]]).astype(bf16)
+                tensor_copy(
+                    RSS.at[s, half, q], RB.at[s, half, chip], rssem.at[s, half, 0],
+                    rssem.at[s, half, 1], 2 * q + core).start()
+            loop(1, 8, part)
+
+        send_parts(0)
         t = mm(attended, AO[...])
         TOS[s] = pack_rank(t).astype(bf16)
         loop(1, 8, lambda k: tensor_copy(
             TOS.at[s], TOR.at[s, chip], tosem.at[s, 0], tosem.at[s, 1],
             lax.rem(me + 2 * k, T)).start())
         TOR[s, chip] = TOS[s]
-        RB[s, chip] = jnp.zeros((64, CHUNK), bf16)
-        y = mm(attended, WO[chip])
-        y = y + ST[s, me].astype(f32)
+        send_parts(1)
+        bases = []
+        for half in range(2):
+            own = ST[me, :, halves[half]] if s == 0 else SG[me, half]
+            bases.append(mm(attended, WO[chip, :, halves[half]]) + own.astype(f32))
         wait(TOR.at[s, pl.ds(0, 7)], tosem.at[s, 1])
-        rank = jnp.sum(TOR[s].astype(f32), axis=0)
-        y = y + low_rank_scale * mm(unpack_split(rank), BO[...])
-        wait(RB.at[s, pl.ds(0, 7)], rssem.at[s, 1])
-        for q in range(8):
-            y = y + RB[s, q].astype(f32)
-        y = y.astype(bf16)
-
+        rank = unpack_split(jnp.sum(TOR[s].astype(f32), axis=0))
+        parts = []
+        for half in range(2):
+            y = bases[half] + low_rank_scale * mm(rank, BO[:, halves[half]])
+            RB[s, half, chip] = jnp.zeros((64, CHUNK // 2), bf16)
+            wait(RB.at[s, half, pl.ds(0, 7)], rssem.at[s, half, 1])
+            for q in range(8):
+                y = y + RB[s, half, q].astype(f32)
+            y = y.astype(bf16)
+            parts.append(y)
+            if s + 1 < STEPS:
+                SG[me, half] = y
+                if half == 1:
+                    squares = [x.astype(f32) * x.astype(f32) for x in parts]
+                    squares = (squares[0][:, 0:128] + squares[0][:, 128:256]) + (
+                        squares[1][:, 0:128] + squares[1][:, 128:256])
+                    SQS[...] = jnp.zeros_like(SQS)
+                    SQS[0:1, 0:64] = jnp.sum(squares.T, axis=0, keepdims=True)
+                    loop(1, T, lambda k: tensor_copy(
+                        SQS, SQR.at[me], sqsem.at[0], sqsem.at[1], lax.rem(me + k, T)).start())
+                loop(1, 8, lambda k: tensor_copy(
+                    SG.at[me, half], SG.at[me, half], agdsem.at[0, half, k],
+                    agdsem.at[1, half, k], lax.rem(me + 2 * k, T)).start())
         if s + 1 < STEPS:
-            ST[1, me] = y
-            squares = y.astype(f32) * y.astype(f32)
-            squares = (squares[:, 0:128] + squares[:, 128:256]) + (
-                squares[:, 256:384] + squares[:, 384:512])
-            SQS[...] = jnp.zeros_like(SQS)
-            SQS[0:1, 0:64] = jnp.sum(squares.T, axis=0, keepdims=True)
-            loop(1, T, lambda k: tensor_copy(
-                SQS, SQR.at[me], sqsem.at[0], sqsem.at[1], lax.rem(me + k, T)).start())
-            loop(1, 8, lambda k: tensor_copy(
-                ST.at[1, me], ST.at[1, me], agdsem.at[0, k], agdsem.at[1, k],
-                lax.rem(me + 2 * k, T)).start())
-            tensor_copy(
-                ST.at[1, me], ST.at[1, me], agfsem.at[0, 0], agfsem.at[1, 0], sib).start()
+            tensor_copy(SG.at[me], SG.at[me], agfsem.at[0, 0], agfsem.at[1, 0], sib).start()
+        y = jnp.concatenate(parts, axis=1)
         yf = y.astype(f32)
         for c in range(4):
             for i in range(4):
@@ -410,19 +422,21 @@
 
             def take(j, carry):
                 q, new = carry
-                NB[j] = (ST[1, j].astype(f32) * inv * gain[j]).astype(bf16)
+                x = jnp.concatenate([SG[j, 0], SG[j, 1]], axis=1).astype(f32)
+                NB[j] = (x * inv * gain[j]).astype(bf16)
                 return project(j, q), project_kv(j, new)
 
             def pass_on_stream(k):
                 j = own_side(k)
-                wait(ST.at[1, j], agdsem.at[1, k])
+                for half in range(2):
+                    wait(SG.at[j, half], agdsem.at[1, half, k])
                 tensor_copy(
-                    ST.at[1, j], ST.at[1, j], agfsem.at[0, k], agfsem.at[1, k], sib).start()
+                    SG.at[j], SG.at[j], agfsem.at[0, k], agfsem.at[1, k], sib).start()
 
             loop(1, 8, pass_on_stream)
             carry = lax.fori_loop(
                 0, 8, lambda k, c: take(own_side(k), c), (zero_query, zero_total), unroll=4)
-            loop(0, 8, lambda k: wait(ST.at[1, other_side(k)], agfsem.at[1, k]))
+            loop(0, 8, lambda k: wait(SG.at[other_side(k)], agfsem.at[1, k]))
             q, new = lax.fori_loop(
                 0, 8, lambda k, c: take(other_side(k), c), carry, unroll=4)
 
@@ -438,9 +452,11 @@
         wait(QR.at[s, pl.ds(0, T - 1)], qsem.at[s, 0])
         wait(AR.at[s, pl.ds(0, T - 1)], asem.at[s, 0])
         wait(TOR.at[s, pl.ds(0, 7)], tosem.at[s, 0])
-        wait(RB.at[s, pl.ds(0, 7)], rssem.at[s, 0])
-    loop(1, 8, lambda k: wait(ST.at[1, me], agdsem.at[0, k]))
-    loop(0, 8, lambda k: wait(ST.at[1, me], agfsem.at[0, k]))
+        for half in range(2):
+            wait(RB.at[s, half, pl.ds(0, 7)], rssem.at[s, half, 0])
+    for half in range(2):
+        loop(1, 8, lambda k: wait(SG.at[me, half], agdsem.at[0, half, k]))
+    loop(0, 8, lambda k: wait(SG.at[me], agfsem.at[0, k]))
     wait(SQR.at[pl.ds(0, T - 1)], sqsem.at[0])
 
 
@@ -476,7 +492,8 @@
             V((8, 2 * CHUNK, CHUNK), bf16),
             V((4, KV_HEADS, CAP, 2, HEAD_DIM), bf16),
             V((4, 64, 128), f32),
-            V((2, T, 64, CHUNK), bf16),
+            V((T, 64, CHUNK), bf16),
+            V((T, 2, 64, CHUNK // 2), bf16),
             V((T, 64, CHUNK), bf16),
             V((128, 128), f32),
             V((128, 128), bf16),
@@ -505,8 +522,8 @@
             V((64, 2 * CHUNK), bf16),
             V((STEPS, 32, 128), bf16),
             V((STEPS, 8, 32, 128), bf16),
-            V((STEPS, 8, 64, CHUNK), bf16),
-            V((STEPS, 8, 64, CHUNK), bf16),
+            V((STEPS, 2, 8, 64, CHUNK // 2), bf16),
+            V((STEPS, 2, 8, 64, CHUNK // 2), bf16),
             V((4, 64, 128), f32),
             V((8, 128), f32),
             V((T, 8, 128), f32),
@@ -523,8 +540,8 @@
             dma((STEPS, 2)),
             dma((STEPS, 2)),
             dma((STEPS, 2)),
-            dma((STEPS, 2)),
-            dma((2, 8)),
+            dma((STEPS, 2, 2)),
+            dma((2, 2, 8)),
             dma((2, 8)),
             dma((2,)),
         ],

time: 93.9 us -> 90.8 us (0.967)
  Pallas kernels: 92.2 us -> 89.1 us
    pallas_call x1, Pallas kernels: 92.2 us -> 89.1 us  [body(): pl.pallas_call(kernel, out_shape=jax.ShapeDtypeStruct((STEPS, 64, CHUNK),...]
where the time goes in v8:
time: 90.8 us; the launch traced here: 90.7 us
  Pallas kernels  89.1 us (98%)
  local copies, waits for them, and re-layouts  1.57 us (2%)
    pallas_call x1, Pallas kernels, body(): pl.pallas_call(kernel, out_shape=jax.ShapeDtypeStruct((STEPS, 64, CHUNK),...  89.1 us

profile of v8, /device:TPU:1, one launch (start us, length us, event | category | flops | bytes accessed | tf_op | source)
XLA Modules:
  0.0 90.7 jit_solution(16231791340014966047)
XLA Ops:
  0.0 89.1 %shard_map.109 = bf16[2,64,512]{2,1,0:T(8,128)(2,1)} custom-call(bf16[64,8192]{1,0:T(8,128)(2,1)} %hid.1, f32[16,1,512]{2,1,0:T(1,128)} %bitcast.8, bf16[32,256,512]{2,1,0:T(8,128)(2,1)} %bitcast.5, bf16[64,8192]{1,0:T(8,128)(2,1)} %bitcast.6, bf16[64,8192]{1,0:T(8,128)(2,1)} %bitcast.7, bf16[512,8192]{1,0:T(8,128)(2,1)} %wo.1, ...), custom_call_target="tpu_custom_call" | custom-call | flops 5000000000 | bytes 26214400 | tf_op jit(solution)/shard_map/pallas_call | solution.py:484
  89.1 1.6 %copy.13 = bf16[2,64,512]{2,1,0:T(8,128)(2,1)} copy(bf16[2,64,512]{2,1,0:T(8,128)(2,1)} %shard_map.109) | data formatting | bytes 262144

commit v9 on v8

--- a/solution.py
+++ b/solution.py
@@ -403,8 +403,9 @@
                 loop(1, 8, lambda k: tensor_copy(
                     SG.at[me, half], SG.at[me, half], agdsem.at[0, half, k],
                     agdsem.at[1, half, k], lax.rem(me + 2 * k, T)).start())
-        if s + 1 < STEPS:
-            tensor_copy(SG.at[me], SG.at[me], agfsem.at[0, 0], agfsem.at[1, 0], sib).start()
+                tensor_copy(
+                    SG.at[me, half], SG.at[me, half], agfsem.at[0, half, 0],
+                    agfsem.at[1, half, 0], sib).start()
         y = jnp.concatenate(parts, axis=1)
         yf = y.astype(f32)
         for c in range(4):
@@ -414,31 +415,38 @@
             out[s, :, 128 * c:128 * c + 128] = OUTF[c].astype(bf16)
 
         if s + 1 < STEPS:
+            def pass_on_stream(half):
+                def pass_on(k):
+                    j = own_side(k)
+                    wait(SG.at[j, half], agdsem.at[1, half, k])
+                    tensor_copy(
+                        SG.at[j, half], SG.at[j, half], agfsem.at[0, half, k],
+                        agfsem.at[1, half, k], sib).start()
+                loop(1, 8, pass_on)
+
+            pass_on_stream(0)
             SQR[me] = SQS[...]
             wait(SQR.at[pl.ds(0, T - 1)], sqsem.at[1])
             total = jnp.sum(SQR[...], axis=0)[0:1]
             total = jnp.broadcast_to(total, (128, 128)).T[0:64, 0:1]
             inv = lax.rsqrt(total * (1.0 / D) + norm_epsilon)
 
-            def take(j, carry):
+            def take(j, half, carry):
                 q, new = carry
-                x = jnp.concatenate([SG[j, 0], SG[j, 1]], axis=1).astype(f32)
-                NB[j] = (x * inv * gain[j]).astype(bf16)
-                return project(j, q), project_kv(j, new)
-
-            def pass_on_stream(k):
-                j = own_side(k)
-                for half in range(2):
-                    wait(SG.at[j, half], agdsem.at[1, half, k])
-                tensor_copy(
-                    SG.at[j], SG.at[j], agfsem.at[0, k], agfsem.at[1, k], sib).start()
-
-            loop(1, 8, pass_on_stream)
-            carry = lax.fori_loop(
-                0, 8, lambda k, c: take(own_side(k), c), (zero_query, zero_total), unroll=4)
-            loop(0, 8, lambda k: wait(SG.at[other_side(k)], agfsem.at[1, k]))
-            q, new = lax.fori_loop(
-                0, 8, lambda k, c: take(other_side(k), c), carry, unroll=4)
+                x = (SG[j, half].astype(f32) * inv * gain[j, :, halves[half]]).astype(bf16)
+                columns = pl.ds(pl.multiple_of(CHUNK * j + 256 * half, 256), 256)
+                return q + mm(x, WQ[2 * j + half]), new + mm_t(x, WKV[:, columns])
+
+            carry = (zero_query, zero_total)
+            for half in range(2):
+                if half == 1:
+                    pass_on_stream(1)
+                carry = lax.fori_loop(
+                    0, 8, lambda k, c: take(own_side(k), half, c), carry, unroll=4)
+                loop(0, 8, lambda k: wait(SG.at[other_side(k), half], agfsem.at[1, half, k]))
+                carry = lax.fori_loop(
+                    0, 8, lambda k, c: take(other_side(k), half, c), carry, unroll=4)
+            q, new = carry
 
     wait(A1R.at[pl.ds(0, 3)], a1sem.at[0, 0])
     wait(A1R.at[pl.ds(0, 4)], a1sem.at[0, 1])
@@ -456,7 +464,7 @@
             wait(RB.at[s, half, pl.ds(0, 7)], rssem.at[s, half, 0])
     for half in range(2):
         loop(1, 8, lambda k: wait(SG.at[me, half], agdsem.at[0, half, k]))
-    loop(0, 8, lambda k: wait(SG.at[me], agfsem.at[0, k]))
+        loop(0, 8, lambda k: wait(SG.at[me, half], agfsem.at[0, half, k]))
     wait(SQR.at[pl.ds(0, T - 1)], sqsem.at[0])
 
 
@@ -542,7 +550,7 @@
             dma((STEPS, 2)),
             dma((STEPS, 2, 2)),
             dma((2, 2, 8)),
-            dma((2, 8)),
+            dma((2, 2, 8)),
             dma((2,)),
         ],
         compiler_params=pltpu.CompilerParams(

time: 90.8 us -> 90.7 us (level)
  no operation moved by 1% of the time
where the time goes in v9:
time: 90.7 us; the launch traced here: 90.5 us
  Pallas kernels  88.9 us (98%)
  local copies, waits for them, and re-layouts  1.57 us (2%)
    pallas_call x1, Pallas kernels, body(): pl.pallas_call(kernel, out_shape=jax.ShapeDtypeStruct((STEPS, 64, CHUNK),...  88.9 us

profile of v9, /device:TPU:1, one launch (start us, length us, event | category | flops | bytes accessed | tf_op | source)
XLA Modules:
  0.0 90.5 jit_solution(3347725164330784027)
XLA Ops:
  0.0 88.9 %shard_map.109 = bf16[2,64,512]{2,1,0:T(8,128)(2,1)} custom-call(bf16[64,8192]{1,0:T(8,128)(2,1)} %hid.1, f32[16,1,512]{2,1,0:T(1,128)} %bitcast.8, bf16[32,256,512]{2,1,0:T(8,128)(2,1)} %bitcast.5, bf16[64,8192]{1,0:T(8,128)(2,1)} %bitcast.6, bf16[64,8192]{1,0:T(8,128)(2,1)} %bitcast.7, bf16[512,8192]{1,0:T(8,128)(2,1)} %wo.1, ...), custom_call_target="tpu_custom_call" | custom-call | flops 5000000000 | bytes 26214400 | tf_op jit(solution)/shard_map/pallas_call | solution.py:492
  89.0 1.6 %copy.13 = bf16[2,64,512]{2,1,0:T(8,128)(2,1)} copy(bf16[2,64,512]{2,1,0:T(8,128)(2,1)} %shard_map.109) | data formatting | bytes 262144

commit v10 on v9

--- a/solution.py
+++ b/solution.py
@@ -202,10 +202,14 @@
     for s in range(8):
         FL[pl.ds(s, 128, stride=8), :] = mm(place, XF[pl.ds(s, 128, stride=8), :].astype(bf16))
     spread_pairs(FL[0:256, :], AE)
-    AQ[me] = (AE[0:256, :] + swap_halves(AE[256:512, :])).astype(bf16)
-    loop(1, 8, lambda k: tensor_copy(
-        AQ.at[me], AQ.at[me], a3dsem.at[0, k], a3dsem.at[1, k], lax.rem(me + 2 * k, T)).start())
-    tensor_copy(AQ.at[me], AQ.at[me], a3fsem.at[0, 0], a3fsem.at[1, 0], sib).start()
+    for r in range(2):
+        AQ[me, r] = (AE[128 * r:128 * r + 128, :] + swap_halves(
+            AE[256 + 128 * r:384 + 128 * r, :])).astype(bf16)
+        loop(1, 8, lambda k: tensor_copy(
+            AQ.at[me, r], AQ.at[me, r], a3dsem.at[0, r, k], a3dsem.at[1, r, k],
+            lax.rem(me + 2 * k, T)).start())
+        tensor_copy(
+            AQ.at[me, r], AQ.at[me, r], a3fsem.at[0, r, 0], a3fsem.at[1, r, 0], sib).start()
     for c in range(4):
         up = (low_rank_scale * FL[pl.ds(256 + c, 64, stride=4), :]).astype(bf16)
         none = jnp.zeros_like(up)
@@ -218,13 +222,13 @@
         BO[64:128, 128 * c:128 * c + 128] = up
     AOS[...] = FL[512:768, :].astype(bf16).reshape(8, 32, 128)
 
-    def merge(j):
+    def merge(j, r):
         strip = pl.ds(pl.multiple_of(16 * j, 16), 16)
         for half in range(2):
-            blocks = pl.ds(16 * half, 16)
+            blocks = pl.ds(16 * half + 8 * r, 8)
             for n in range(2):
                 columns = slice(256 * n, 256 * n + 256)
-                change = mm(AQ[j], BQ[half, :, columns]).reshape(16, 16, 256)
+                change = mm(AQ[j, r], BQ[half, :, columns]).reshape(8, 16, 256)
                 WQ[blocks, strip, columns] = (
                     WQ[blocks, strip, columns].astype(f32) + change).astype(bf16)
 
@@ -234,10 +238,13 @@
     def other_side(k):
         return lax.rem(sib + T - 2 * k, T)
 
-    def pass_on_strips(k):
-        j = own_side(k)
-        wait(AQ.at[j], a3dsem.at[1, k])
-        tensor_copy(AQ.at[j], AQ.at[j], a3fsem.at[0, k], a3fsem.at[1, k], sib).start()
+    def pass_on_strips(r):
+        def pass_on(k):
+            j = own_side(k)
+            wait(AQ.at[j, r], a3dsem.at[1, r, k])
+            tensor_copy(
+                AQ.at[j, r], AQ.at[j, r], a3fsem.at[0, r, k], a3fsem.at[1, r, k], sib).start()
+        loop(1, 8, pass_on)
 
     wait(KV, lsem.at[19])
 
@@ -247,12 +254,14 @@
         KEYS[i, g] = DI[pl.ds(0, CAP, stride=2), :].astype(bf16)
         VALS[i, g] = DI[pl.ds(1, CAP, stride=2), :].astype(bf16)
 
-    merge(me)
+    merge(me, 0)
+    merge(me, 1)
     loop(0, 4 * KV_HEADS, part_cache)
-    loop(1, 8, pass_on_strips)
-    loop(1, 8, lambda k: merge(own_side(k)))
-    loop(0, 8, lambda k: wait(AQ.at[other_side(k)], a3fsem.at[1, k]))
-    loop(0, 8, lambda k: merge(other_side(k)))
+    for r in range(2):
+        pass_on_strips(r)
+        loop(1, 8, lambda k: merge(own_side(k), r))
+        loop(0, 8, lambda k: wait(AQ.at[other_side(k), r], a3fsem.at[1, r, k]))
+        loop(0, 8, lambda k: merge(other_side(k), r))
 
     low_half = lanes((8, 128)) < 64
     sub = lax.broadcasted_iota(jnp.int32, (8, 128), 0) & 3
@@ -453,8 +462,9 @@
     wait(WO.at[:, pl.ds(0, CHUNK), :], wosem.at[0])
     for half in range(2):
         wait(A2R.at[0, pl.ds(0, T - 1)], a2sem.at[half, 0])
-    loop(1, 8, lambda k: wait(AQ.at[me], a3dsem.at[0, k]))
-    loop(0, 8, lambda k: wait(AQ.at[me], a3fsem.at[0, k]))
+    for r in range(2):
+        loop(1, 8, lambda k: wait(AQ.at[me, r], a3dsem.at[0, r, k]))
+        loop(0, 8, lambda k: wait(AQ.at[me, r], a3fsem.at[0, r, k]))
     wait(AOR.at[pl.ds(0, T - 1)], aosem.at[0])
     for s in range(STEPS):
         wait(QR.at[s, pl.ds(0, T - 1)], qsem.at[s, 0])
@@ -511,7 +521,7 @@
             V((1024, 128), f32),
             V((T, 32, 128), f32),
             V((512, 128), f32),
-            V((T, 256, 128), bf16),
+            V((T, 2, 128, 128), bf16),
             V((2, 128, CHUNK), bf16),
             V((128, CHUNK), bf16),
             V((8, 32, 128), bf16),
@@ -542,8 +552,8 @@
             dma((2,)),
             dma((2, 2)),
             dma((2, 2)),
-            dma((2, 8)),
-            dma((2, 8)),
+            dma((2, 2, 8)),
+            dma((2, 2, 8)),
             dma((2,)),
             dma((STEPS, 2)),
             dma((STEPS, 2)),

time: 90.7 us -> 91.5 us (level)
  no operation moved by 1% of the time
where the time goes in v10:
time: 91.5 us; the launch traced here: 91.4 us
  Pallas kernels  89.8 us (98%)
  local copies, waits for them, and re-layouts  1.57 us (2%)
    pallas_call x1, Pallas kernels, body(): pl.pallas_call(kernel, out_shape=jax.ShapeDtypeStruct((STEPS, 64, CHUNK),...  89.8 us

profile of v10, /device:TPU:1, one launch (start us, length us, event | category | flops | bytes accessed | tf_op | source)
XLA Modules:
  0.0 91.4 jit_solution(3332546419377893872)
XLA Ops:
  0.0 89.8 %shard_map.109 = bf16[2,64,512]{2,1,0:T(8,128)(2,1)} custom-call(bf16[64,8192]{1,0:T(8,128)(2,1)} %hid.1, f32[16,1,512]{2,1,0:T(1,128)} %bitcast.8, bf16[32,256,512]{2,1,0:T(8,128)(2,1)} %bitcast.5, bf16[64,8192]{1,0:T(8,128)(2,1)} %bitcast.6, bf16[64,8192]{1,0:T(8,128)(2,1)} %bitcast.7, bf16[512,8192]{1,0:T(8,128)(2,1)} %wo.1, ...), custom_call_target="tpu_custom_call" | custom-call | flops 5000000000 | bytes 26214400 | tf_op jit(solution)/shard_map/pallas_call | solution.py:502
  89.8 1.6 %copy.13 = bf16[2,64,512]{2,1,0:T(8,128)(2,1)} copy(bf16[2,64,512]{2,1,0:T(8,128)(2,1)} %shard_map.109) | data formatting | bytes 262144

commit v11 on v9

--- a/solution.py
+++ b/solution.py
@@ -103,11 +103,6 @@
             wq.at[pl.ds(4 * j, 4)], WQ.at[pl.ds(4 * j, 4)], lsem.at[0]).start()
     pltpu.make_async_copy(wk_t, WKV.at[pl.ds(0, 64), :], lsem.at[16]).start()
     pltpu.make_async_copy(wv_t, WKV.at[pl.ds(64, 64), :], lsem.at[17]).start()
-    for i in range(4):
-        for g in range(KV_HEADS):
-            pltpu.make_async_copy(
-                kv.at[i, :, :, pl.ds(HEAD_DIM * g, HEAD_DIM)], KV.at[i, g], lsem.at[19]).start()
-
     def wo_columns(q, parity):
         return wo.at[:, pl.ds(pl.multiple_of((2 * q + parity) * CHUNK, CHUNK), CHUNK)]
 
@@ -140,6 +135,10 @@
     loop(1, 4, lambda k: send_piece(lax.rem(ro + 2 * k, R), 0))
     other = ro + 1 - 2 * lax.rem(ro, 2)
     loop(0, 4, lambda k: send_piece(lax.rem(other + 2 * k, R), 1))
+    for i in range(4):
+        for g in range(KV_HEADS):
+            pltpu.make_async_copy(
+                kv.at[i, :, :, pl.ds(HEAD_DIM * g, HEAD_DIM)], KV.at[i, g], lsem.at[19]).start()
     loop(0, 8, lambda q: tensor_copy(
         wo_columns(q, 1 - core), WO.at[q, wo_rows, :], wosem.at[0], wosem.at[1], sib).start())
 

time: 90.7 us -> 90.7 us (level)
  no operation moved by 1% of the time
where the time goes in v11:
time: 90.7 us; the launch traced here: 90.5 us
  Pallas kernels  88.9 us (98%)
  local copies, waits for them, and re-layouts  1.57 us (2%)
    pallas_call x1, Pallas kernels, body(): pl.pallas_call(kernel, out_shape=jax.ShapeDtypeStruct((STEPS, 64, CHUNK),...  88.9 us

profile of v11, /device:TPU:1, one launch (start us, length us, event | category | flops | bytes accessed | tf_op | source)
XLA Modules:
  0.0 90.5 jit_solution(13587237604837745530)
XLA Ops:
  0.0 88.9 %shard_map.109 = bf16[2,64,512]{2,1,0:T(8,128)(2,1)} custom-call(bf16[64,8192]{1,0:T(8,128)(2,1)} %hid.1, f32[16,1,512]{2,1,0:T(1,128)} %bitcast.8, bf16[32,256,512]{2,1,0:T(8,128)(2,1)} %bitcast.5, bf16[64,8192]{1,0:T(8,128)(2,1)} %bitcast.6, bf16[64,8192]{1,0:T(8,128)(2,1)} %bitcast.7, bf16[512,8192]{1,0:T(8,128)(2,1)} %wo.1, ...), custom_call_target="tpu_custom_call" | custom-call | flops 5000000000 | bytes 26214400 | tf_op jit(solution)/shard_map/pallas_call | solution.py:491
  89.0 1.6 %copy.13 = bf16[2,64,512]{2,1,0:T(8,128)(2,1)} copy(bf16[2,64,512]{2,1,0:T(8,128)(2,1)} %shard_map.109) | data formatting | bytes 262144

commit v12 on v9

--- a/solution.py
+++ b/solution.py
@@ -266,7 +266,7 @@
             return q + mm(NB[j], WQ[pl.ds(2 * j, 2)].reshape(CHUNK, CHUNK))
 
         if s == 0:
-            q = lax.fori_loop(0, T, project, zero_query, unroll=4)
+            q = lax.fori_loop(0, T, project, zero_query, unroll=8)
         for h in range(4):
             Q32[64 * h:64 * h + 64, :] = q[:, 128 * h:128 * h + 128]
         Q32[256:320, :] = new

time: 90.7 us -> 90.4 us (level)
  no operation moved by 1% of the time
where the time goes in v12:
time: 90.4 us; the launch traced here: 90.2 us
  Pallas kernels  88.7 us (98%)
  local copies, waits for them, and re-layouts  1.57 us (2%)
    pallas_call x1, Pallas kernels, body(): pl.pallas_call(kernel, out_shape=jax.ShapeDtypeStruct((STEPS, 64, CHUNK),...  88.7 us

profile of v12, /device:TPU:1, one launch (start us, length us, event | category | flops | bytes accessed | tf_op | source)
XLA Modules:
  0.0 90.2 jit_solution(5439694593003242043)
XLA Ops:
  0.0 88.7 %shard_map.109 = bf16[2,64,512]{2,1,0:T(8,128)(2,1)} custom-call(bf16[64,8192]{1,0:T(8,128)(2,1)} %hid.1, f32[16,1,512]{2,1,0:T(1,128)} %bitcast.8, bf16[32,256,512]{2,1,0:T(8,128)(2,1)} %bitcast.5, bf16[64,8192]{1,0:T(8,128)(2,1)} %bitcast.6, bf16[64,8192]{1,0:T(8,128)(2,1)} %bitcast.7, bf16[512,8192]{1,0:T(8,128)(2,1)} %wo.1, ...), custom_call_target="tpu_custom_call" | custom-call | flops 5000000000 | bytes 26214400 | tf_op jit(solution)/shard_map/pallas_call | solution.py:492
  88.7 1.6 %copy.13 = bf16[2,64,512]{2,1,0:T(8,128)(2,1)} copy(bf16[2,64,512]{2,1,0:T(8,128)(2,1)} %shard_map.109) | data formatting | bytes 262144
